TPU v7x, 32 devices: a whole 2x2x4 slice. The times are simulated.
32 devices in a mesh: group: 2 (over y), shot: 4 (over z), line: 2 (over x), tm: 2 (over core).
Axes of the slice: x: 2, y: 2, z: 4, core: 2. Of those that a mesh axis runs over, the one named last changes fastest.
Arguments:
- initial_guess: bfloat16 [8, 256, 1024], P(('group', 'shot'), 'line', 'tm'), parts along dimension 0
- measured_mixtures: bfloat16 [4, 256, 1024], P('group', 'line'), parts along dimension 0
- launch_lags: int32 [8], P('group'), parts along dimension 0, may hold values from 0 to 127, as said below
- source_launch_order: int32 [8], P('group'), parts along dimension 0, may hold values from 0 to 3, each once
- station_portion_tallies: int32 [16], P('group'), parts along dimension 0, may hold values from 1 to 32, 128 in all
- source_entry_kernel: bfloat16 [4, 3, 64], replicated, may hold values from -1.75 to 1.75
- source_spaced_kernel: bfloat16 [3, 64, 64], replicated, may hold values from -0.4375 to 0.4375
- source_exit_kernel: bfloat16 [4, 64], replicated, may hold values from -0.5 to 0.5
- source_inner_offsets: float32 [2, 64], replicated, may hold values from -3 to 3
- station_entry_kernel: bfloat16 [4, 3, 64], replicated, may hold values from -1.75 to 1.75
- station_spaced_kernel: bfloat16 [3, 64, 64], replicated, may hold values from -0.4375 to 0.4375
- station_exit_kernel: bfloat16 [4, 64], replicated, may hold values from -0.5 to 0.5
- station_inner_offsets: float32 [2, 64], replicated, may hold values from -3 to 3
- learned_pace_factors: float32 [2], replicated, may hold values from 0.3 to 0.8
Outputs:
- deblended: bfloat16 [8, 256, 1024], P(('group', 'shot'), 'line', 'tm'), parts along dimension 0
There are 2 independent parts, one for each index of `group`. A program takes and returns all parts, laid end to end along the dimension named above; an argument that names none is the same for every part. Nothing has to cross between parts.
Inputs may be any that keep to these rules, and one draw needn't show every extreme that they name: `launch_lags`: 0 and 127 both occur. `source_launch_order`: each shot once. `station_portion_tallies`: the counts sum to 128 and the largest equals 32.
All inputs are finite; a program needn't handle non-finite values.
Results may differ from a plain program's by a relative error of at most 0.013.
Values may be sent and summed in bfloat16 or wider, within the bound.
A program may use at most 64 MiB of HBM per device.

v0:
```python
import functools
import math

import jax
import jax.numpy as jnp
import numpy as np
from jax import lax
from jax.experimental import pallas as pl
from jax.experimental.pallas import tpu as pltpu
from jax.sharding import PartitionSpec as P

RPL = 16
ITERS = 2
EPSILON = 1e-05
C = 8
PACK = 4
TAPS = (1, 2, 3, 0)
F32, BF16 = jnp.float32, jnp.bfloat16
AXES = ("shot", "line", "tm")


def ahead(x, k):
    edge = pltpu.roll(x[:k], C - 1, 1)
    edge = jnp.where(lax.broadcasted_iota(jnp.int32, edge.shape, 1) == C - 1, 0.0, edge)
    return edge if k == x.shape[0] else jnp.concatenate([x[k:], edge], axis=0)


def behind(x, k):
    edge = pltpu.roll(x[x.shape[0] - k :], 1, 1)
    edge = jnp.where(lax.broadcasted_iota(jnp.int32, edge.shape, 1) == 0, 0.0, edge)
    return edge if k == x.shape[0] else jnp.concatenate([edge, x[: x.shape[0] - k]], axis=0)


def even_lanes(shape):
    return lax.broadcasted_iota(jnp.int32, shape, len(shape) - 1) < shape[-1] // 2


def net(x, w_in, pick, w_mid, w_out, place, bias, total, band):
    planes, _, lanes = x.shape
    rows = planes * C
    side = jnp.where(even_lanes(x.shape), ahead(x, 1), behind(x, 1))
    z = jnp.concatenate([x, side], axis=2).astype(BF16).reshape(rows, 2 * lanes)
    total[...] = jnp.zeros_like(total)
    wide = w_in.shape[1]
    feat = wide // PACK
    for j in range(3):
        tap = w_mid[j].astype(F32)
        for i in range(PACK):
            row = [tap if p == i else jnp.zeros_like(tap) for p in range(PACK)]
            at = (j * PACK + i) * feat
            band[at : at + feat, :] = jnp.concatenate(row, axis=1).astype(BF16)

    def step(q, carry):
        w_here = jnp.dot(pick[q], w_in[...], preferred_element_type=F32).astype(BF16)
        o_here = jnp.dot(w_out[...], place[q], preferred_element_type=F32).astype(BF16)
        h = jnp.dot(z, w_here, preferred_element_type=F32)
        h = jnp.maximum(h + bias[0:1, :], 0.0)
        cube = h.reshape(planes, C, wide)
        first = ahead(cube[:2], 2).reshape(2 * C, wide).astype(BF16)
        last = behind(cube[planes - 2 :], 2).reshape(2 * C, wide).astype(BF16)
        hb = h.astype(BF16)
        early = jnp.concatenate([last, hb[: rows - 2 * C]], axis=0)
        late = jnp.concatenate([hb[2 * C :], first], axis=0)
        g = jnp.dot(jnp.concatenate([early, hb, late], axis=1), band[...], preferred_element_type=F32)
        g = jnp.maximum(g + bias[1:2, :], 0.0).astype(BF16)
        total[...] += jnp.dot(g, o_here, preferred_element_type=F32)
        return carry

    lax.fori_loop(0, pick.shape[0], step, 0, unroll=2)
    y = total[...].reshape(planes, C, 2 * lanes)
    a, b = y[:, :, :lanes], y[:, :, lanes:]
    return a + jnp.where(even_lanes(b.shape), behind(b, 1), ahead(b, 1))


def shot_step(x, weights, member, out_ref, part_ref, total, band):
    y = (x + net(x, *weights, total, band)).astype(BF16)
    out_ref[...] = y
    y = y.astype(F32)
    energy = jnp.sum(jnp.sum(y * y, axis=0), axis=0, keepdims=True)
    sums = jnp.sum(member[...] * energy, axis=1, keepdims=True)
    part_ref[...] = jnp.broadcast_to(sums, part_ref.shape)


def shifted(buf, lag_ref, shots, forward):
    planes, lanes = buf.shape[1] // 2, buf.shape[3]
    shape = (planes, C, lanes)
    even = even_lanes(shape)
    per = lanes // 2 // shots
    lane_shot = lax.rem(lax.broadcasted_iota(jnp.int32, shape, 2), lanes // 2) // per
    out = jnp.zeros(shape, F32)
    for s in range(shots):
        lag = lag_ref[s]
        half, odd = lag // 2, lax.rem(lag, 2)
        at_even = half if forward else planes - half - odd
        at_odd = half + odd if forward else planes - half
        one = jnp.where(even, buf[odd, pl.ds(at_even, planes)], buf[odd, pl.ds(at_odd, planes)])
        out = jnp.where(lane_shot == s, one, out)
    return out


def station_step(shots, sp, tot_ref, spread, weights, lags, join, mix, take, pace, buf, total, band):
    planes, _, lanes = sp.shape
    rows = planes * C
    mean = jnp.sum(tot_ref[:, 0:1] * spread[...], axis=0, keepdims=True)
    rms = jnp.sqrt(mean + EPSILON).reshape(1, 1, lanes)
    normed = (sp / rms).astype(BF16).astype(F32)
    settled = (sp + rms * net(normed, *weights, total, band)).astype(BF16).astype(F32)

    def fill(x, forward):
        far = ahead(x, planes) if forward else behind(x, planes)
        near_at, far_at = (0, planes) if forward else (planes, 0)
        for v, at in ((x, near_at), (far, far_at)):
            buf[0, at : at + planes] = v
            h = lanes // 2
            buf[1, at : at + planes] = jnp.concatenate([v[:, :, h:], v[:, :, :h]], axis=2)

    fill(settled, False)
    fired = shifted(buf, lags, shots, False).astype(BF16).reshape(rows, lanes)
    misfit = jnp.dot(fired, join[...], preferred_element_type=F32)
    misfit -= jnp.dot(mix[...], take[...], preferred_element_type=F32)
    fill(misfit.reshape(planes, C, lanes), True)
    return (settled - pace * shifted(buf, lags, shots, True)).astype(BF16)


def by_phase(width):
    row = lax.broadcasted_iota(jnp.int32, (width, width), 0)
    col = lax.broadcasted_iota(jnp.int32, (width, width), 1)
    half = width // 2
    return jnp.where(col == 2 * lax.rem(row, half) + row // half, 1.0, 0.0).astype(BF16)


def unfold(read, into, sort):
    planes = into.shape[0]
    for c in range(C):
        v = lax.dot_general(sort, read(c), (((1,), (1,)), ((), ())), preferred_element_type=F32)
        into[:, c, :] = jnp.concatenate([v[:planes], v[planes:]], axis=1)


def entry_kernel(
    dims, x, wi, wp, wm, wo, wq, bi, member, out, part, mix, total, band, cube, side
):
    shots, blocks, halves = dims
    width = 2 * cube.shape[0]
    sort, each = by_phase(width), C // halves

    def traces(c):
        at, t = slice(c % each * width, (c % each + 1) * width), c // each
        rows = [x[(s * blocks + b) * halves + t, :, at].astype(F32) for s in range(shots) for b in range(blocks)]
        return jnp.concatenate(rows, axis=0).astype(BF16)

    tl = each * width

    def records(c):
        s, t = c // halves, c % halves
        rows = [
            x[(s * blocks + b) * halves + t, :, tl + g * width : tl + (g + 1) * width].astype(F32)
            for g in range((x.shape[2] - tl) // width)
            for b in range(blocks)
        ]
        return jnp.concatenate(rows, axis=0).astype(BF16)

    unfold(records, side, sort)
    mix[...] = side[...].astype(BF16).reshape(mix.shape)
    unfold(traces, cube, sort)
    shot_step(cube[...], (wi, wp, wm, wo, wq, bi), member, out, part, total, band)


def exit_kernel(
    it, dims, lags, pace, sp, tot, spread, wi, wp, wm, wo, wq, bi, join, mix, take, out, buf, total, band, cube
):
    shots, blocks, halves = dims
    width = 2 * cube.shape[0]
    sort, each = by_phase(width), C // halves
    x = station_step(
        shots, sp[...].astype(F32), tot, spread, (wi, wp, wm, wo, wq, bi), lags, join, mix, take, pace[it], buf, total, band
    )
    cube[...] = x.astype(F32)
    n, lh = cube.shape[2] // 2, out.shape[1]
    for c in range(C):
        v = cube[:, c, :]
        v = jnp.concatenate([v[:, :n], v[:, n:]], axis=0).T.astype(BF16)
        v = jnp.dot(v, sort, preferred_element_type=F32)
        at, t = slice(c % each * width, (c % each + 1) * width), c // each
        for j in range(shots * blocks):
            out[j * halves + t, :, at] = v[j * lh : (j + 1) * lh].astype(BF16)


def first_kernel(x, wi, wp, wm, wo, wq, bi, member, out, part, total, band):
    shot_step(x[...].astype(F32), (wi, wp, wm, wo, wq, bi), member, out, part, total, band)


def station_kernel(it, shots, lags, pace, sp, tot, spread, wi, wp, wm, wo, wq, bi, join, mix, take, out, buf, total, band):
    out[...] = station_step(
        shots, sp[...].astype(F32), tot, spread, (wi, wp, wm, wo, wq, bi), lags, join, mix, take, pace[it], buf, total, band
    )


def both_kernel(
    it, shots, lags, pace, sp, tot, spread, wi, wp, wm, wo, wq, bi, join, mix, take, vi, vp, vm, vo, vq, ci, member, out, part, buf, total, band
):
    x = station_step(
        shots, sp[...].astype(F32), tot, spread, (wi, wp, wm, wo, wq, bi), lags, join, mix, take, pace[it], buf, total, band
    )
    shot_step(x.astype(F32), (vi, vp, vm, vo, vq, ci), member, out, part, total, band)


def call(body, outs, ins, smem, scratch):
    v, s = pl.BlockSpec(memory_space=pltpu.VMEM), pl.BlockSpec(memory_space=pltpu.SMEM)
    return pl.pallas_call(
        body,
        out_shape=outs,
        in_specs=[s] * smem + [v] * (len(ins) - smem),
        out_specs=jax.tree.map(lambda _: v, outs),
        scratch_shapes=scratch,
        compiler_params=pltpu.CompilerParams(vmem_limit_bytes=48 * 2**20),
    )(*ins)


def prepared(w_in, w_mid, w_out, bias, near):
    n, feat = near.shape[1], w_in.shape[2]
    tiles = n // PACK
    cols = near.reshape(3, n, tiles, PACK).transpose(2, 1, 0, 3)
    pick = np.einsum("jk,tnci->tjnkci", np.eye(4)[list(TAPS)], cols).reshape(tiles, 4 * n, 12 * PACK)
    place = np.einsum("kj,tin->tjikn", np.eye(4)[list(TAPS)], np.eye(n).reshape(tiles, PACK, n)).reshape(tiles, 4 * PACK, 4 * n)
    w1 = w_in.reshape(12, 1, 1, feat)
    eye = jnp.eye(PACK, dtype=BF16)
    rows = (w1 * eye[None, :, :, None]).reshape(12 * PACK, PACK * feat)
    w2 = w_out.T.reshape(1, feat, 4, 1)
    ends = (w2 * eye[:, None, None, :]).reshape(PACK * feat, 4 * PACK)
    return rows, jnp.asarray(pick, BF16), w_mid, ends, jnp.asarray(place, BF16), jnp.tile(bias, (1, PACK))


def exchange_kernel(sizes, x, out, slots, send, recv):
    count = math.prod(sizes)
    me = (lax.axis_index("shot") * sizes[1] + lax.axis_index("line")) * sizes[2] + lax.axis_index("tm")

    def peer(off):
        at = lax.rem(me + off, count)
        return {
            "shot": at // (sizes[1] * sizes[2]),
            "line": lax.rem(at // sizes[2], sizes[1]),
            "tm": lax.rem(at, sizes[2]),
        }

    barrier = pltpu.get_barrier_semaphore()
    for off in range(1, count):
        pl.semaphore_signal(barrier, inc=1, device_id=peer(off), device_id_type=pl.DeviceIdType.MESH)
    pl.semaphore_wait(barrier, count - 1)
    copies = []
    for off in range(1, count):
        copy = pltpu.make_async_remote_copy(
            src_ref=x,
            dst_ref=slots.at[off],
            send_sem=send.at[off],
            recv_sem=recv.at[off],
            device_id=peer(off),
            device_id_type=pl.DeviceIdType.MESH,
        )
        copy.start()
        copies.append(copy)
    total = x[...]
    for off, copy in enumerate(copies, 1):
        copy.wait()
        total += slots[off]
    out[...] = total


def summed(x, sizes):
    count, v = math.prod(sizes), pl.BlockSpec(memory_space=pltpu.VMEM)
    return pl.pallas_call(
        functools.partial(exchange_kernel, sizes),
        out_shape=jax.ShapeDtypeStruct(x.shape, x.dtype),
        in_specs=[v],
        out_specs=v,
        scratch_shapes=[
            pltpu.VMEM((count, *x.shape), x.dtype),
            pltpu.SemaphoreType.DMA((count,)),
            pltpu.SemaphoreType.DMA((count,)),
        ],
        compiler_params=pltpu.CompilerParams(collective_id=0, has_side_effects=True),
    )(x)


def per_device(guess, mixtures, lags, order, tallies, e1, m1, x1, b1, e2, m2, x2, b2, pace):
    sh, recv, tl = guess.shape
    n_shot, n_line, n_tm = (lax.axis_size(a) for a in AXES)
    whole = RPL % (n_shot * n_line * n_tm) == 0
    where = AXES if whole else AXES[1:]
    parts = math.prod(lax.axis_size(a) for a in where)
    kp, lh = RPL // parts, recv // RPL
    lines, shots, nt = lh * n_line, sh * n_shot, tl * n_tm
    planes, s1 = nt // 2 // C, shots if whole else sh
    r1 = lines * kp
    r2 = r1 if whole else r1 // n_shot
    lanes1, lanes2 = 2 * s1 * r1, 2 * shots * r2
    sources = n_shot if whole else 1
    i32 = functools.partial(jnp.arange, dtype=jnp.int32)

    at_shot = lax.axis_index("shot")
    n_mix, run = mixtures.shape[0], nt // C
    fused = whole and sh == 1 and kp == 1 and C % n_tm == 0 and n_shot * n_tm == C
    x = guess.reshape(sh, lh, parts, kp, tl).transpose(2, 0, 1, 3, 4)
    if fused:
        share = (at_shot * n_tm + lax.axis_index("tm")) * run
        mine = lax.dynamic_slice_in_dim(mixtures, share, run, axis=2).reshape(n_mix, lh, parts, run)
        mine = mine.transpose(2, 1, 0, 3).reshape(parts, lh, n_mix * run)
        x = jnp.concatenate([x.reshape(parts, lh, tl), mine], axis=2)
    x = lax.all_to_all(x, where, split_axis=0, concat_axis=0, tiled=False)
    if not fused:
        x = x.reshape(sources, n_line, n_tm, sh, lh, kp, tl).transpose(0, 3, 1, 4, 5, 2, 6)
        x = x.reshape(s1, r1, C, planes, 2).transpose(3, 2, 4, 0, 1).reshape(planes, C, lanes1)


    def first_k(line):
        block = line * n_tm + lax.axis_index("tm")
        return (at_shot * n_line * n_tm + block if whole else block) * kp

    if not fused:
        grid = mixtures.reshape(n_mix, lh, RPL, nt)
        sent = jnp.stack([lax.dynamic_slice_in_dim(grid, first_k(d), kp, axis=2) for d in range(n_line)])
        m = lax.all_to_all(sent, "line", split_axis=0, concat_axis=0)
        m = m.transpose(1, 0, 2, 3, 4).reshape(n_mix, r1, nt)
        if not whole:
            m = lax.dynamic_slice_in_dim(m, at_shot * r2, r2, axis=1)
        m = m.reshape(n_mix, r2, C, planes, 2).transpose(3, 2, 4, 0, 1).reshape(planes * C, 2 * n_mix * r2)

    np_ = tallies.shape[0]
    here = i32(np_)
    offsets = jnp.sum(jnp.where(here[None, :] < here[:, None], tallies[None, :], 0), axis=1)
    mine = first_k(lax.axis_index("line"))

    def one_hot(r):
        line, k = r // kp, mine + lax.rem(r, kp)
        q = lax.rem(line, lh) * RPL + k
        inside = (offsets[:, None] <= q[None, :]) & (q[None, :] < (offsets + tallies)[:, None])
        block = (line // lh)[None, :] == i32(n_line)[:, None]
        return (block[:, None, :] & inside[None, :, :]).reshape(n_line * np_, r.shape[0]).astype(F32)

    member = jnp.tile(one_hot(i32(r1)), (1, 2 * s1))
    r_own = i32(r2) if whole else at_shot * r2 + i32(r2)
    count = jnp.tile((tallies * (shots * nt)).astype(F32), n_line)
    spread = jnp.tile(one_hot(r_own) / count[:, None], (1, 2 * shots))

    sid = i32(shots)
    place = jnp.sum(jnp.where(order[None, :] == sid[:, None], sid[None, :], 0), axis=1)
    group = place // (shots // n_mix)
    same = (group[:, None] == group[None, :]).astype(BF16)
    chosen = (i32(n_mix)[:, None] == group[None, :]).astype(BF16)
    rest, two = jnp.eye(r2, dtype=BF16), jnp.eye(2, dtype=BF16)
    join = jnp.kron(two, jnp.kron(same, rest))
    take = jnp.kron(two, jnp.kron(chosen, rest))

    n1, n2 = s1 * r1, shots * r2
    a, b = np.arange(n1)[:, None], np.arange(n1)[None, :]
    near1 = np.stack([(a == b + (c - 1) * kp) & (a // r1 == b // r1) for c in range(3)])
    a, b = np.arange(n2)[:, None], np.arange(n2)[None, :]
    near2 = np.stack([a == b + (c - 1) * r2 for c in range(3)])
    wa = prepared(e1, m1, x1, b1, near1)
    wb = prepared(e2, m2, x2, b2, near2)

    rows = planes * C
    tot1, tot2 = pltpu.VMEM((rows, 2 * lanes1), F32), pltpu.VMEM((rows, 2 * lanes2), F32)
    feat = e1.shape[2]
    band = pltpu.VMEM((3 * PACK * feat, PACK * feat), BF16)
    buf = pltpu.VMEM((2, 2 * planes, C, lanes2), F32)
    spass = jax.ShapeDtypeStruct((planes, C, lanes1), BF16)
    part = jax.ShapeDtypeStruct((n_line * np_, 128), F32)
    moved = jax.ShapeDtypeStruct((planes, C, lanes2), BF16)

    def to_stations(y):
        y = y.reshape(rows, 2, sh, n_shot, r2)
        y = lax.all_to_all(y, "shot", split_axis=3, concat_axis=2, tiled=True)
        return y.reshape(planes, C, lanes2)

    def to_shots(y):
        y = y.reshape(rows, 2, shots, 1, r2)
        y = lax.all_to_all(y, "shot", split_axis=2, concat_axis=3, tiled=True)
        return y.reshape(planes, C, lanes1)

    dims = (n_shot, n_line, n_tm)
    cube = pltpu.VMEM((planes, C, lanes1), F32)
    if fused:
        mixed = jax.ShapeDtypeStruct((rows, 2 * n_mix * r2), BF16)
        side = pltpu.VMEM((planes, C, 2 * n_mix * r2), F32)
        sp, energy, m = call(
            functools.partial(entry_kernel, dims),
            (spass, part, mixed),
            (x, *wa, member),
            0,
            [tot1, band, cube, side],
        )
    else:
        sp, energy = call(first_kernel, (spass, part), (x, *wa, member), 0, [tot1, band])
    for it in range(ITERS):
        tot = summed(energy, (n_shot, n_line, n_tm)) if whole else lax.psum(energy, AXES)
        if not whole:
            sp = to_stations(sp)
        ins = (lags, pace, sp, tot, spread, *wb, join, m, take)
        if whole and it < ITERS - 1:
            sp, energy = call(
                functools.partial(both_kernel, it, shots), (spass, part), (*ins, *wa, member), 2, [buf, tot2, band]
            )
            continue
        if fused:
            back = jax.ShapeDtypeStruct((parts, lh, tl), BF16)
            x = call(functools.partial(exit_kernel, it, dims), back, ins, 2, [buf, tot2, band, cube])
            continue
        x = call(functools.partial(station_kernel, it, shots), moved, ins, 2, [buf, tot2, band])
        if not whole:
            x = to_shots(x)
            if it < ITERS - 1:
                sp, energy = call(first_kernel, (spass, part), (x, *wa, member), 0, [tot1, band])

    if not fused:
        x = x.reshape(planes, C, 2, s1, r1).transpose(3, 4, 1, 0, 2)
        x = x.reshape(sources, sh, n_line, lh, kp, n_tm, tl).transpose(0, 2, 5, 1, 3, 4, 6)
    x = lax.all_to_all(x.reshape(parts, sh, lh, kp, tl), where, split_axis=0, concat_axis=0)
    return x.transpose(1, 2, 0, 3, 4).reshape(sh, recv, tl)


def solution(mesh):
    spec = P(("group", "shot"), "line", "tm")
    placed = (spec, P("group", "line", None), P("group"), P("group"), P("group")) + (P(),) * 9
    return jax.shard_map(per_device, mesh=mesh, in_specs=placed, out_specs=spec, check_vma=False)
```

profile of v0, /device:TPU:0, one launch (start us, length us, event | category | flops | bytes accessed | tf_op | source)
XLA Modules:
  0.0 121.0 jit_solution(15744677346640708935)
XLA Ops:
  0.0 1.0 copy-done
  1.1 0.9 copy-done.15
  2.1 0.7 pad_maximum_fusion
  2.7 7.4 %all-to-all-start = ((bf16[16,8,768]{2,1,0:T(8,128)(2,1)}), bf16[16,8,768]{2,1,0:T(8,128)(2,1)S(1)}, u32[]{:S(2)}, u32[]{:S(2)}) async-start(bf16[16,8,768]{2,1,0:T(8,128)(2,1)} %pad_maximum_fusion), calls=%async_computation | async-start | bytes 393216 | tf_op jit(solution)/shard_map/all_to_all | solution.py:308
  10.2 0.1 select_reduce_fusion.1
  10.4 0.1 select_reduce_fusion
  10.7 0.1 copy.45
  10.9 0.1 broadcast_multiply_fusion.2
  11.0 0.1 mul.204.wi.vi
  11.1 0.6 copy-done.19
  11.7 0.1 copy-done.18
  12.0 0.1 copy.46.wo.vo
  12.1 0.6 copy-done.20
  12.7 0.7 tile.19.bi.ci
  13.8 0.1 broadcast_multiply_fusion
  14.4 0.1 mul.216.wi
  14.6 0.1 copy.48.wo
  14.8 0.7 tile.50.bi
  15.4 3.7 %all-to-all-done.x = bf16[16,8,768]{2,1,0:T(8,128)(2,1)S(1)} async-done(((bf16[16,8,768]{2,1,0:T(8,128)(2,1)}), bf16[16,8,768]{2,1,0:T(8,128)(2,1)S(1)}, u32[]{:S(2)}, u32[]{:S(2)}) %all-to-all-start) | async-done | bytes 196640 | tf_op jit(solution)/shard_map/all_to_all | solution.py:308
  19.1 0.7 copy-done.8
  19.8 16.8 %shard_map.172 = (bf16[64,8,128]{2,1,0:T(8,128)(2,1)S(1)}, f32[16,128]{1,0:T(8,128)S(1)}, bf16[512,64]{1,0:T(8,128)(2,1)S(1)}) custom-call(bf16[16,8,768]{2,1,0:T(8,128)(2,1)S(1)} %all-to-all-done.x, bf16[48,256]{1,0:T(8,128)(2,1)S(1)} %mul.204.wi.vi, bf16[16,256,48]{2,1,0:T(8,128)(2,1)S(1)} %copy-done.2, bf16[3,64,64]{2,1,0:T(8,128)(2,1)S(1)} %copy-done.4, ...), custom_call_target="tpu_custom_call" | custom-call | tf_op jit(solution)/shard_map/pallas_call | solution.py:209
  36.6 0.6 copy-done.12
  37.2 8.1 %shard_map.173.tot = f32[16,128]{1,0:T(8,128)} custom-call(f32[16,128]{1,0:T(8,128)} %copy-done.12), custom_call_target="tpu_custom_call" | custom-call | tf_op jit(solution)/shard_map/pallas_call | solution.py:270
  45.4 0.6 copy-done.9
  46.0 0.7 copy-done.7
  46.7 33.6 %shard_map.174 = (bf16[64,8,128]{2,1,0:T(8,128)(2,1)S(1)}, f32[16,128]{1,0:T(8,128)S(1)}) custom-call(s32[4]{0:T(128)S(1)} %copy-done.13, f32[2]{0:T(128)S(1)} %copy-done.14, bf16[64,8,128]{2,1,0:T(8,128)(2,1)S(1)} %get-tuple-element.10.sp, f32[16,128]{1,0:T(8,128)S(1)} %copy-done.7, f32[16,128]{1,0:T(8,128)S(1)} %tile.48.spread, ...), custom_call_target="tpu_custom_call" | custom-call | tf_op jit(solution)/shard_map/pallas_call | solution.py:209
  80.4 0.6 copy-done.11
  81.0 8.1 %shard_map.175.tot = f32[16,128]{1,0:T(8,128)} custom-call(f32[16,128]{1,0:T(8,128)} %copy-done.11), custom_call_target="tpu_custom_call" | custom-call | tf_op jit(solution)/shard_map/pallas_call | solution.py:270
  89.1 0.7 copy-done.6
  89.8 17.7 %shard_map.176 = bf16[16,8,512]{2,1,0:T(8,128)(2,1)S(1)} custom-call(s32[4]{0:T(128)S(1)} %copy-done.13, f32[2]{0:T(128)S(1)} %copy-done.14, bf16[64,8,128]{2,1,0:T(8,128)(2,1)S(1)} %get-tuple-element.13.sp, f32[16,128]{1,0:T(8,128)S(1)} %copy-done.6, f32[16,128]{1,0:T(8,128)S(1)} %tile.48.spread, bf16[48,256]{1,0:T(8,128)(2,1)S(1)} %mul.216.wi, ...), custom_call_target="tpu_custom_call" | custom-call | tf_op jit(solution)/shard_map/pallas_call | solution.py:209
  107.5 12.8 %all_to_all.10 = bf16[16,1,8,1,512]{4,2,3,1,0:T(8,128)(2,1)S(1)} all-to-all(bf16[16,1,8,1,512]{4,2,3,1,0:T(8,128)(2,1)S(1)} %bitcast.28), channel_id=1, replica_groups=mesh['group'=2,'shot'=4,'line'=2,'tm'=2] {'shot','line','tm'}, dimensions={0} | all-to-all | bytes 262144 | tf_op jit(solution)/shard_map/all_to_all | solution.py:417
  120.3 0.7 copy.52
  (75 shorter events, 1.7 us)
Async XLA Ops:
  0.0 1.0 copy-start
  1.0 0.9 copy-start.15
  1.9 8.2 %copy-start.23 = (s32[4]{0:T(128)S(1)}, s32[4]{0:T(128)}, u32[]{:S(2)}) copy-start(s32[4]{0:T(128)} %param.21) | copy-start | bytes 52
  1.9 8.4 %copy-start.22 = (s32[8]{0:T(128)S(1)}, s32[8]{0:T(128)}, u32[]{:S(2)}) copy-start(s32[8]{0:T(128)} %param.22) | copy-start | bytes 100
  2.0 8.9 %copy-start.16 = (bf16[4,3,64]{2,0,1:T(4,128)(2,1)S(1)}, bf16[4,3,64]{2,0,1:T(4,128)(2,1)}, u32[]{:S(2)}) copy-start(bf16[4,3,64]{2,0,1:T(4,128)(2,1)} %param.23) | copy-start | bytes 4612
  2.0 8.9 %copy-start.17 = (bf16[4,3,64]{2,0,1:T(4,128)(2,1)S(1)}, bf16[4,3,64]{2,0,1:T(4,128)(2,1)}, u32[]{:S(2)}) copy-start(bf16[4,3,64]{2,0,1:T(4,128)(2,1)} %param.27) | copy-start | bytes 4612
  2.0 17.1 %copy-start.2 = (bf16[16,256,48]{2,1,0:T(8,128)(2,1)S(1)}, bf16[16,256,48]{2,1,0:T(8,128)(2,1)}, u32[]{:S(2)}) copy-start(bf16[16,256,48]{2,1,0:T(8,128)(2,1)} %constant.73.clone.wp.vp) | copy-start | bytes 1179652
  2.7 16.4 %all-to-all-start = ((bf16[16,8,768]{2,1,0:T(8,128)(2,1)}), bf16[16,8,768]{2,1,0:T(8,128)(2,1)S(1)}, u32[]{:S(2)}, u32[]{:S(2)}) async-start(bf16[16,8,768]{2,1,0:T(8,128)(2,1)} %pad_maximum_fusion), calls=%async_computation | async-start | bytes 393216 | tf_op jit(solution)/shard_map/all_to_all | solution.py:308
  11.0 0.7 copy-start.19
  11.1 0.7 copy-start.18
  12.0 0.7 copy-start.20
  13.6 1.2 copy-start.21
  13.7 5.4 %copy-start.3 = (bf16[16,16,256]{2,1,0:T(8,128)(2,1)S(1)}, bf16[16,16,256]{2,1,0:T(8,128)(2,1)}, u32[]{:S(2)}) copy-start(bf16[16,16,256]{2,1,0:T(8,128)(2,1)} %constant.74.clone.wq.vq) | copy-start | bytes 393220
  13.7 5.4 %copy-start.4 = (bf16[3,64,64]{2,1,0:T(8,128)(2,1)S(1)}, bf16[3,64,64]{2,1,0:T(8,128)(2,1)}, u32[]{:S(2)}) copy-start(bf16[3,64,64]{2,1,0:T(8,128)(2,1)} %vm.1) | copy-start | bytes 73732
  13.8 31.6 %copy-start.1 = (bf16[16,256,48]{2,1,0:T(8,128)(2,1)S(1)}, bf16[16,256,48]{2,1,0:T(8,128)(2,1)}, u32[]{:S(2)}) copy-start(bf16[16,256,48]{2,1,0:T(8,128)(2,1)} %constant.75.clone.wp) | copy-start | bytes 1179652
  19.1 0.7 copy-start.8
  19.8 25.6 %copy-start.5 = (bf16[3,64,64]{2,1,0:T(8,128)(2,1)S(1)}, bf16[3,64,64]{2,1,0:T(8,128)(2,1)}, u32[]{:S(2)}) copy-start(bf16[3,64,64]{2,1,0:T(8,128)(2,1)} %wm.5) | copy-start | bytes 73732
  36.6 0.6 copy-start.12
  37.2 8.2 %copy-start.10 = (f32[2,256]{1,0:T(2,128)S(1)}, f32[2,256]{1,0:T(2,128)}, u32[]{:S(2)}) copy-start(f32[2,256]{1,0:T(2,128)} %tile.50.bi) | copy-start | bytes 6148
  45.3 0.7 copy-start.9
  45.4 0.7 copy-start.13
  45.4 0.7 copy-start.14
  46.0 0.7 copy-start.7
  80.3 0.6 copy-start.11
  89.1 0.7 copy-start.6
where the time goes:
time: 122 us; the launch traced here: 121 us
  Pallas kernels  84.4 us (69%)
  blocking collectives  12.8 us (10%)
  local copies, waits for them, and re-layouts  10.6 us (9%)
  starting transfers between devices  7.36 us (6%)
  waiting for transfers between devices  3.67 us (3%)
  other arithmetic  1.81 us (1%)
    pallas_call x3, Pallas kernels, call(): pl.pallas_call(body, out_shape=outs, in_specs=[s] * smem + [v] * (len(ins...  68.2 us
    pallas_call x2, Pallas kernels, summed(): pl.pallas_call(functools.partial(exchange_kernel, sizes), out_shape=jax.S...  16.2 us
    all_to_all x1, blocking collectives, per_device(): lax.all_to_all(x.reshape(parts, sh, lh, kp, tl), where, split_axis=0, con...  12.8 us
    all_to_all x1, starting transfers between devices, per_device(): x = lax.all_to_all(x, where, split_axis=0, concat_axis=0, tiled=False)  7.36 us
    unnamed x50, local copies, waits for them, and re-layouts  7.08 us
    all_to_all x1, waiting for transfers between devices, per_device(): x = lax.all_to_all(x, where, split_axis=0, concat_axis=0, tiled=False)  3.67 us
  transfers between devices with their start and end apart: 1, of which 1 were waited for; matrix products, arithmetic and copies ran while one was open for 3% of the time, Pallas kernels for 0%

commit v1 on v0

--- a/solution.py
+++ b/solution.py
@@ -281,6 +281,435 @@
     )(x)
 
 
+SLOT = (0, 3, 1, 2)
+HALF = 64
+GROUPS = 4
+
+
+def iota(shape, dim):
+    return lax.broadcasted_iota(jnp.int32, shape, dim)
+
+
+def weave(w_in, w_mid, w_out, bias, we, wm, wo, bi):
+    feat = w_in.shape[2]
+    wide = feat * len(SLOT)
+    row, lane = iota((wide, wide), 0), iota((wide, wide), 1)
+    at, ch = lax.rem(row, HALF), row // HALF
+    slot = lane // feat
+    pos = jnp.where(slot == 1, 3, jnp.where(slot == 0, 0, slot - 1))
+    taps = w_in[...].astype(F32)
+    for par in range(2):
+        turned = lax.rem(at + (1 if par == 0 else HALF - 1), HALF)
+        tap = lax.rem(turned, 4)
+        base = jnp.zeros((wide, wide), F32)
+        for c in range(3):
+            for t in range(4):
+                line = jnp.concatenate([taps[t, c : c + 1, :]] * len(SLOT), axis=1)
+                base = jnp.where((ch == c) & (tap == t), line, base)
+        for g in range(GROUPS):
+            we[par * GROUPS + g] = jnp.where(turned // 4 == 4 * g + pos, base, 0.0).astype(BF16)
+    zero = jnp.zeros((feat, feat), F32)
+    mid = [w_mid[j].astype(F32) for j in range(3)]
+
+    def block(came, goes):
+        j = came - goes + 1
+        return mid[j] if came is not None and 0 <= j < 3 else zero
+
+    for n, came in enumerate(SLOT + (4, None, None, -1)):
+        blocks = [zero if came is None else block(came, goes) for goes in SLOT]
+        wm[n * feat : (n + 1) * feat, :] = jnp.concatenate(blocks, axis=1).astype(BF16)
+
+    def sample(shape):
+        col = iota(shape, 1)
+        m = lax.rem(col, HALF)
+        edge = jnp.where(m == HALF - 1, -1, jnp.where(m == 0, HALF, -4 * HALF))
+        return jnp.where(col >= 2 * HALF, edge, m)
+
+    near, far = sample((4, wide)), sample((feat, wide))
+    for par in range(2):
+        pick = jnp.where(lax.rem(near - 2 * par + 1 + 8 * HALF, 4) == iota((4, wide), 0), 1.0, 0.0).astype(BF16)
+        base = lax.dot_general(w_out[...], pick, (((0,), (0,)), ((), ())), preferred_element_type=F32)
+        for g in range(GROUPS):
+            for n, i in enumerate(SLOT):
+                d = far - 4 * (4 * g + i) - 2 * par + 1
+                at = ((par * GROUPS + g) * len(SLOT) + n) * feat
+                wo[at : at + feat, :] = jnp.where((d >= 0) & (d < 4), base, 0.0).astype(BF16)
+    bi[...] = jnp.concatenate([bias[...]] * len(SLOT), axis=1)
+
+
+def layers(zs, hs, gs, ys, we, wm, wo, bi):
+    b0, b1 = bi[0:1, :], bi[1:2, :]
+    rows, wide = zs.shape[1:]
+    blocks = ys.shape[0] - 2
+    per = rows // blocks
+    for par in range(2):
+        for g in range(GROUPS):
+            h = jnp.dot(zs[par], we[par * GROUPS + g], preferred_element_type=F32)
+            h = jnp.maximum(h + b0, 0.0).astype(BF16)
+            for b in range(blocks):
+                at = per + (b * GROUPS + g) * per
+                hs[par, at : at + per, :] = h[b * per : (b + 1) * per]
+    for par in range(2):
+        for r in range(0, GROUPS * rows, rows):
+            at = per + r
+            x = [hs[par, at : at + rows, :]]
+            x += [hs[par, at + d : at + d + rows, : wide // 2] for d in (per, -per)]
+            g = jnp.dot(jnp.concatenate(x, axis=1), wm[...], preferred_element_type=F32)
+            g = jnp.maximum(g + b1, 0.0).astype(BF16)
+            for n in range(rows // per):
+                b, q = divmod(r // per + n, GROUPS)
+                col = (par * GROUPS + q) * wide
+                gs[b * per : (b + 1) * per, col : col + wide] = g[n * per : (n + 1) * per]
+    y = jnp.dot(gs[...], wo[...], preferred_element_type=F32)
+    ys[1 : 1 + blocks] = y.reshape(blocks, per, wide)
+
+
+def widen(pn, zs):
+    blocks, per, wide = pn.shape
+    lane = lax.rem(iota((per, wide), 1), HALF)
+
+    def step(b, carry):
+        here = pn[b + 1]
+        at = pl.ds(pl.multiple_of(b * per, per), per)
+        zs[0, at, :] = jnp.where(lane == HALF - 1, pn[b], here).astype(BF16)
+        zs[1, at, :] = jnp.where(lane == 0, pn[b + 2], here).astype(BF16)
+        return carry
+
+    lax.fori_loop(0, blocks - 2, step, 0)
+
+
+def patch_kernel(sizes, lags, order, tallies, pace, guess, mixtures, *refs):
+    wa, wb, out = refs[:4], refs[4:8], refs[8]
+    (gbuf, mbuf, sendx, recvx, sendm, recvm, backs, backr, sende, recve) = refs[9:19]
+    (xs, mx, rolled, mf, member, pn, zs, hs, gs, ys) = refs[19:29]
+    ta, tb = refs[29:33], refs[33:37]
+    load_sem, ssem, rsem = refs[37:]
+    n_shot, n_line, n_tm = sizes
+    count = math.prod(sizes)
+    at_shot, at_line, at_tm = (lax.axis_index(a) for a in AXES)
+    me = (at_shot * n_line + at_line) * n_tm + at_tm
+    shots = n_shot
+    n_mix = mixtures.shape[0]
+    run = shots // n_mix
+    lc = guess.shape[1] // count
+    tl = guess.shape[2]
+    tile = 2 * HALF
+    blocks = tl * n_tm // HALF
+    each = tl // HALF
+
+    def device(at):
+        return {"shot": at // (n_line * n_tm), "line": lax.rem(at // n_tm, n_line), "tm": lax.rem(at, n_tm)}
+
+    barrier = pltpu.get_barrier_semaphore()
+    for off in range(1, count):
+        pl.semaphore_signal(barrier, inc=1, device_id=device(lax.rem(me + off, count)), device_id_type=pl.DeviceIdType.MESH)
+    loads = [
+        pltpu.make_async_copy(guess.at[0], gbuf, load_sem.at[0]),
+        pltpu.make_async_copy(mixtures, mbuf, load_sem.at[1]),
+    ]
+    for copy in loads:
+        copy.start()
+    for ref in (hs, ys, pn, rolled, mf):
+        ref[...] = jnp.zeros_like(ref)
+
+    def send(which, src, dst, to):
+        return pltpu.make_async_remote_copy(
+            src_ref=src,
+            dst_ref=dst,
+            send_sem=ssem.at[which, to],
+            recv_sem=rsem.at[which, me],
+            device_id=device(to),
+            device_id_type=pl.DeviceIdType.MESH,
+        )
+
+    def arrival(which, src, dst, came):
+        return pltpu.make_async_remote_copy(
+            src_ref=src,
+            dst_ref=dst,
+            send_sem=ssem.at[which, came],
+            recv_sem=rsem.at[which, came],
+            device_id=device(came),
+            device_id_type=pl.DeviceIdType.MESH,
+        )
+
+    recv_n = guess.shape[1]
+    row, col = iota((recv_n, recv_n), 0), iota((recv_n, recv_n), 1)
+    perm = jnp.where(col == lax.rem(row, lc) * count + row // lc, 1.0, 0.0).astype(BF16)
+    loads[0].wait()
+    v = jnp.dot(perm, gbuf[...], preferred_element_type=F32)
+    for k in range(count):
+        part = v[k * lc : (k + 1) * lc]
+        sendx[k] = jnp.concatenate([part[:, : tl // 2], part[:, tl // 2 :]], axis=0).astype(BF16)
+    loads[1].wait()
+    other = (at_shot * n_line + (n_line - 1 - at_line)) * n_tm + at_tm
+    row, col = iota((2 * lc, recv_n), 0), iota((2 * lc, recv_n), 1)
+    wanted = jnp.where(row < lc, me, other)
+    pick = jnp.where(col == lax.rem(row, lc) * count + wanted, 1.0, 0.0).astype(BF16)
+    picked = [jnp.dot(pick, mbuf[g], preferred_element_type=F32) for g in range(n_mix)]
+    recvm[at_line] = jnp.concatenate([p[:lc] for p in picked], axis=0).astype(BF16)
+    sendm[...] = jnp.concatenate([p[lc:] for p in picked], axis=0).astype(BF16)
+    recvx[me] = sendx[me]
+
+    pl.semaphore_wait(barrier, count - 1)
+    for off in range(1, count):
+        to = lax.rem(me + off, count)
+        send(0, sendx.at[to], recvx.at[me], to).start()
+    send(1, sendm, recvm.at[at_line], other).start()
+
+    weave(*wa, *ta)
+    weave(*wb, *tb)
+    sec = []
+    for rows in ((lc, tile), (count, tile)):
+        if rows[0] == lc:
+            q = iota(rows, 0) * count + me
+        else:
+            q = lax.rem(iota(rows, 1), lc) * count + iota(rows, 0)
+        edge, at, size = jnp.int32(0), jnp.zeros(rows, jnp.int32), jnp.zeros(rows, jnp.int32)
+        for p in range(tallies.shape[0]):
+            at = jnp.where(q >= edge, p, at)
+            size = jnp.where(q >= edge, tallies[p], size)
+            edge = edge + tallies[p]
+        sec.append((at, size))
+    for k in range(count):
+        member[k] = jnp.where(sec[0][0] == sec[1][0][k : k + 1, :], 1.0, 0.0)
+    scale = 1.0 / (sec[0][1] * (shots * tl * n_tm)).astype(F32)
+
+    lane = iota((lc, tile), 1)
+    low = lane < HALF
+    inner = lax.rem(lane, HALF)
+
+    def wait_all(which, src, dst, ids):
+        for came in ids:
+            arrival(which, src(came), dst(came), came).wait_recv()
+
+    def sent_all(which, src, dst, ids):
+        for to in ids:
+            send(which, src(to), dst(to), to).wait_send()
+
+    peers = [lax.rem(me + off, count) for off in range(1, count)]
+    wait_all(0, lambda p: sendx.at[p], lambda p: recvx.at[p], peers)
+
+    def unfold(v):
+        turned = pltpu.roll(v, HALF, 1)
+        return jnp.where(low, v, turned), jnp.where(low, turned, v)
+
+    for p in range(count):
+        s, l, t = p // (n_line * n_tm), p // n_tm % n_line, p % n_tm
+        v = recvx[p].astype(F32)
+        top = (l * shots + s) * lc
+        for j in range(tl // tile):
+            h, c = divmod(j * tile, tl // 2)
+            two = unfold(v[h * lc : (h + 1) * lc, c : c + tile])
+            for n in range(2):
+                xs[t * each + 2 * j + n, top : top + lc, :] = two[n]
+    arrival(1, sendm, recvm.at[n_line - 1 - at_line], other).wait_recv()
+    for l in range(n_line):
+        v = recvm[l].astype(F32)
+        for g in range(n_mix):
+            for j in range(blocks // 2):
+                two = unfold(v[g * lc : (g + 1) * lc, j * tile : (j + 1) * tile])
+                for n in range(2):
+                    mx[2 * j + n, g * n_line + l] = two[n]
+
+    per = n_line * shots * lc
+    cube = (n_line * shots, lc, tile)
+    clow = lax.rem(iota(cube, 2), 2 * HALF) < HALF
+    line_of = iota(cube, 1)
+    early = lax.rem(iota((per, tile), 1), HALF) < HALF // 2
+
+    def beside(before, here, after):
+        both = jnp.where(clow, before, here)
+        return jnp.concatenate([both.reshape(per, tile), after.reshape(per, tile)], axis=1)
+
+    def change(b):
+        return ys[b + 1, :, :tile] + jnp.where(early, ys[b, :, tile:], ys[b + 2, :, tile:])
+
+    none = jnp.zeros((shots, lc, tile), F32)
+    one = none[:1]
+    group = []
+    for s in range(shots):
+        found = jnp.int32(0)
+        for k in range(shots):
+            found = jnp.where(order[k] == s, k // run, found)
+        group.append(found)
+    rest = [lax.rem(lags[s], HALF) for s in range(shots)]
+
+    def iterate(it, carry):
+        def lines(b, carry):
+            x = xs[b].reshape(cube)
+            down, up = pltpu.roll(x, 1, 1), pltpu.roll(x, lc - 1, 1)
+            before = jnp.where(line_of == 0, jnp.concatenate([none, down[: per // lc - shots]], axis=0), down)
+            after = jnp.where(line_of == lc - 1, jnp.concatenate([up[shots:], none], axis=0), up)
+            pn[b + 1] = beside(before, x, after)
+            return carry
+
+        lax.fori_loop(0, blocks, lines, 0)
+        widen(pn, zs)
+        layers(zs, hs, gs, ys, *ta)
+
+        def passed(b, energy):
+            x = (xs[b] + change(b)).astype(BF16).astype(F32)
+            xs[b] = x
+            return energy + jnp.sum((x * x).reshape(n_line, shots, lc, tile), axis=1)
+
+        energy = lax.fori_loop(0, blocks, passed, jnp.zeros((n_line, lc, tile), F32))
+        mine = jnp.zeros((lc, tile), F32)
+        for l in range(n_line):
+            e = 0.5 * jnp.sum(energy[l], axis=1, keepdims=True)
+            mine = mine + jnp.where(lane == iota((lc, tile), 0) + l * lc, e, 0.0)
+        mine = jnp.sum(mine, axis=0, keepdims=True)
+        sende[it] = mine
+        recve[it, me] = mine
+        for to in peers:
+            send(2 + it, sende.at[it], recve.at[it, me], to).start()
+        wait_all(2 + it, lambda p: sende.at[it], lambda p: recve.at[it, p], peers)
+        sent_all(2 + it, lambda p: sende.at[it], lambda p: recve.at[it, me], peers)
+        total = jnp.zeros((lc, tile), F32)
+        for k in range(count):
+            total = total + member[k] * recve[it, k]
+        total = total * scale
+        rms, inv = [], []
+        for l in range(n_line):
+            mean = jnp.sum(jnp.where(lane // lc == l, total, 0.0), axis=1, keepdims=True)
+            root = jnp.broadcast_to(jnp.sqrt(mean + EPSILON), (lc, tile)).reshape(1, lc, tile)
+            rms += [root] * shots
+            inv += [1.0 / root] * shots
+        rms, inv = jnp.concatenate(rms, axis=0), jnp.concatenate(inv, axis=0)
+
+        def stations(b, carry):
+            x = (xs[b].reshape(cube) * inv).astype(BF16).astype(F32)
+            before, after = [], []
+            for l in range(n_line):
+                at = x[l * shots : (l + 1) * shots]
+                before += [one, at[: shots - 1]]
+                after += [at[1:], one]
+            pn[b + 1] = beside(jnp.concatenate(before, axis=0), x, jnp.concatenate(after, axis=0))
+            return carry
+
+        lax.fori_loop(0, blocks, stations, 0)
+        widen(pn, zs)
+        layers(zs, hs, gs, ys, *tb)
+
+        def settle(b, carry):
+            x = xs[b].reshape(cube) + rms * change(b).reshape(cube)
+            x = x.astype(BF16).astype(F32)
+            xs[b] = x.reshape(per, tile)
+            for n in range(n_line * shots):
+                rolled[b + 2, n] = pltpu.roll(x[n], rest[n % shots], 1)
+            return carry
+
+        lax.fori_loop(0, blocks, settle, 0)
+        for g in range(n_mix):
+            for l in range(n_line):
+                acc = -mx[:, g * n_line + l]
+                for i in range(run):
+                    s = order[g * run + i]
+                    lag = lags[s]
+                    a = 2 - lag // HALF
+                    near = rolled[pl.ds(a, blocks), l * shots + s]
+                    far = rolled[pl.ds(a - 1, blocks), l * shots + s]
+                    acc = acc + jnp.where((inner >= lax.rem(lag, HALF))[None], near, far)
+                mf[:blocks, g * n_line + l] = acc
+        for s in range(shots):
+            for l in range(n_line):
+                m = mf[:, group[s] * n_line + l]
+                m = pltpu.roll(m, lax.rem(tile - rest[s], tile), 2)
+                rolled[: blocks + 2, l * shots + s] = m
+        for s in range(shots):
+            for l in range(n_line):
+                a = lags[s] // HALF
+                near = rolled[pl.ds(a, blocks), l * shots + s]
+                far = rolled[pl.ds(a + 1, blocks), l * shots + s]
+                back = jnp.where((inner < HALF - rest[s])[None], near, far)
+                top = (l * shots + s) * lc
+                xs[:, top : top + lc, :] = (xs[:, top : top + lc, :] - pace[it] * back).astype(BF16).astype(F32)
+        rolled[:2] = jnp.zeros_like(rolled[:2])
+        return carry
+
+    lax.fori_loop(0, ITERS, iterate, 0)
+
+    for p in range(count):
+        s, l, t = p // (n_line * n_tm), p // n_tm % n_line, p % n_tm
+        top = (l * shots + s) * lc
+        halves = []
+        for j in range(tl // tile):
+            b = t * each + 2 * j
+            halves.append(jnp.where(low, xs[b, top : top + lc, :], xs[b + 1, top : top + lc, :]))
+        n = len(halves) // 2
+        halves = [jnp.concatenate(halves[:n], axis=1), jnp.concatenate(halves[n:], axis=1)]
+        backs[p] = jnp.concatenate(halves, axis=0).astype(BF16)
+    for to in peers:
+        send(2 + ITERS, backs.at[to], backr.at[me], to).start()
+    backr[me] = backs[me]
+    wait_all(2 + ITERS, lambda p: backs.at[p], lambda p: backr.at[p], peers)
+    v = []
+    for k in range(count):
+        part = backr[k].astype(F32)
+        v.append(jnp.concatenate([part[:lc], part[lc:]], axis=1))
+    v = jnp.concatenate(v, axis=0).astype(BF16)
+    row, col = iota((recv_n, recv_n), 0), iota((recv_n, recv_n), 1)
+    perm = jnp.where(row == lax.rem(col, lc) * count + col // lc, 1.0, 0.0).astype(BF16)
+    out[0] = jnp.dot(perm, v, preferred_element_type=F32).astype(BF16)
+    sent_all(0, lambda p: sendx.at[p], lambda p: recvx.at[me], peers)
+    send(1, sendm, recvm.at[at_line], other).wait_send()
+    sent_all(2 + ITERS, lambda p: backs.at[p], lambda p: backr.at[me], peers)
+
+
+def patch(guess, mixtures, lags, order, tallies, wa, wb, pace, sizes):
+    count = math.prod(sizes)
+    n_shot, n_line, n_tm = sizes
+    recv, tl = guess.shape[1:]
+    n_mix, nt = mixtures.shape[0], mixtures.shape[2]
+    lc, tile = recv // count, 2 * HALF
+    blocks, traces = nt // HALF, n_line * n_shot
+    per, feat = traces * lc, wa[0].shape[2]
+    wide = feat * len(SLOT)
+    rows = blocks * per
+    v, s, h = (pl.BlockSpec(memory_space=m) for m in (pltpu.VMEM, pltpu.SMEM, pl.ANY))
+    slab = pltpu.VMEM((count, 2 * lc, tl // 2), BF16)
+    woven = [
+        pltpu.VMEM((2 * GROUPS, wide, wide), BF16),
+        pltpu.VMEM((2 * wide, wide), BF16),
+        pltpu.VMEM((2 * GROUPS * wide, wide), BF16),
+        pltpu.VMEM((2, wide), F32),
+    ]
+    kinds = 3 + ITERS
+    return pl.pallas_call(
+        functools.partial(patch_kernel, sizes),
+        out_shape=jax.ShapeDtypeStruct(guess.shape, BF16),
+        in_specs=[s] * 4 + [h] * 2 + [v] * 8,
+        out_specs=v,
+        scratch_shapes=[
+            pltpu.VMEM((recv, tl), BF16),
+            pltpu.VMEM(mixtures.shape, BF16),
+            slab,
+            slab,
+            pltpu.VMEM((n_mix * lc, nt), BF16),
+            pltpu.VMEM((n_line, n_mix * lc, nt), BF16),
+            slab,
+            slab,
+            pltpu.VMEM((ITERS, 1, tile), F32),
+            pltpu.VMEM((ITERS, count, 1, tile), F32),
+            pltpu.VMEM((blocks, per, tile), F32),
+            pltpu.VMEM((blocks, n_mix * n_line, lc, tile), F32),
+            pltpu.VMEM((blocks + 2, traces, lc, tile), F32),
+            pltpu.VMEM((blocks + 2, n_mix * n_line, lc, tile), F32),
+            pltpu.VMEM((count, lc, tile), F32),
+            pltpu.VMEM((blocks + 2, per, wide), F32),
+            pltpu.VMEM((2, rows, wide), BF16),
+            pltpu.VMEM((2, GROUPS * rows + 2 * per, wide), BF16),
+            pltpu.VMEM((rows, 2 * GROUPS * wide), BF16),
+            pltpu.VMEM((blocks + 2, per, wide), F32),
+            *woven,
+            *woven,
+            pltpu.SemaphoreType.DMA((2,)),
+            pltpu.SemaphoreType.DMA((kinds, count)),
+            pltpu.SemaphoreType.DMA((kinds, count)),
+        ],
+        compiler_params=pltpu.CompilerParams(vmem_limit_bytes=56 * 2**20, collective_id=1, has_side_effects=True),
+    )(lags, order, tallies, pace, guess, mixtures, *wa, *wb)
+
+
 def per_device(guess, mixtures, lags, order, tallies, e1, m1, x1, b1, e2, m2, x2, b2, pace):
     sh, recv, tl = guess.shape
     n_shot, n_line, n_tm = (lax.axis_size(a) for a in AXES)
@@ -295,6 +724,13 @@
     lanes1, lanes2 = 2 * s1 * r1, 2 * shots * r2
     sources = n_shot if whole else 1
     i32 = functools.partial(jnp.arange, dtype=jnp.int32)
+    n_mix, feat = mixtures.shape[0], e1.shape[2]
+    square = sh == 1 and kp == 1 and n_line == 2 and shots % n_mix == 0 and feat == HALF
+    square = square and lh == C and tl % (4 * HALF) == 0 and n_mix * lh % 16 == 0
+    square = square and lines == parts and 2 * (n_mix // n_line) == n_line
+    if square:
+        sizes = (n_shot, n_line, n_tm)
+        return patch(guess, mixtures, lags, order, tallies, (e1, m1, x1, b1), (e2, m2, x2, b2), pace, sizes)
 
     at_shot = lax.axis_index("shot")
     n_mix, run = mixtures.shape[0], nt // C

time: 122 us -> 58.8 us (0.48)
  Pallas kernels: 84.4 us -> 55.1 us
  blocking collectives: 12.8 us -> 0 us
  starting transfers between devices: 7.36 us -> 0 us
  local copies, waits for them, and re-layouts: 10.6 us -> 3.46 us
  waiting for transfers between devices: 3.67 us -> 0 us
  other arithmetic: 1.81 us -> 0 us
    pallas_call x5 -> x1, Pallas kernels: 84.4 us -> 55.1 us  [patch(): pl.pallas_call(functools.partial(patch_kernel, sizes), out_shape=jax.Shap...]
    all_to_all x1 -> x0, blocking collectives: 12.8 us -> none  [per_device(): lax.all_to_all(x.reshape(parts, sh, lh, kp, tl), where, split_axis=0, con...]
    all_to_all x1 -> x0, starting transfers between devices: 7.36 us -> none  [per_device(): x = lax.all_to_all(x, where, split_axis=0, concat_axis=0, tiled=False)]
    all_to_all x1 -> x0, waiting for transfers between devices: 3.67 us -> none  [per_device(): x = lax.all_to_all(x, where, split_axis=0, concat_axis=0, tiled=False)]
    unnamed x50 -> x5, local copies, waits for them, and re-layouts: 7.08 us -> 3.46 us
    another operation x9 -> x0, local copies, waits for them, and re-layouts: 1.51 us -> none  [the longest x4 1.34 us: prepared(): jnp.tile(bias, (1, PACK))]
  transfers between devices with their start and end apart: 1 -> 0, of which waited for: 1 -> 0; matrix products, arithmetic and copies ran while one was open for 3% -> 0% of each run, Pallas kernels for 0% -> 0%
where the time goes in v1:
time: 58.8 us; the launch traced here: 58.6 us
  Pallas kernels  55.1 us (94%)
  local copies, waits for them, and re-layouts  3.46 us (6%)
    pallas_call x1, Pallas kernels, patch(): pl.pallas_call(functools.partial(patch_kernel, sizes), out_shape=jax.Shap...  55.1 us
    unnamed x5, local copies, waits for them, and re-layouts  3.46 us

profile of v1, /device:TPU:0, one launch (start us, length us, event | category | flops | bytes accessed | tf_op | source)
XLA Modules:
  0.0 58.6 jit_solution(2527146610519284810)
XLA Ops:
  0.0 0.0 copy-start
  0.0 1.3 %copy.15.refs_0_ = bf16[4,3,64]{2,1,0:T(4,128)(2,1)} copy(bf16[4,3,64]{2,0,1:T(4,128)(2,1)} %param.19) | data formatting | bytes 3072 | tf_op args[5]
  1.3 0.0 copy-done
  1.3 0.6 %copy.16.refs_4_ = bf16[4,3,64]{2,1,0:T(4,128)(2,1)} copy(bf16[4,3,64]{2,0,1:T(4,128)(2,1)S(1)} %copy-done) | data formatting | bytes 3072 | tf_op args[9]
  1.9 55.1 %shard_map.136 = bf16[1,128,512]{2,1,0:T(8,128)(2,1)} custom-call(s32[4]{0:T(128)} %lags.1, s32[4]{0:T(128)} %order.1, s32[8]{0:T(128)} %tallies.1, f32[2]{0:T(128)} %pace.1, bf16[1,128,512]{2,1,0:T(8,128)(2,1)} %guess.1, bf16[2,128,1024]{2,1,0:T(8,128)(2,1)} %mixtures.1, bf16[4,3,64]{2,1,0:T(4,128)(2,1)} %copy.15.refs_0_, bf16[3,64,64]{2,1,0:T(8,128)(2,1)} %refs_1_.1, ...), custom_call_target="tpu_custom_call" | custom-call | tf_op jit(solution)/shard_map/pallas_call | solution.py:677
  57.0 1.6 %copy.18 = bf16[1,128,512]{2,1,0:T(8,128)(2,1)} copy(bf16[1,128,512]{2,1,0:T(8,128)(2,1)} %shard_map.136) | data formatting | bytes 262144
Async XLA Ops:
  0.0 1.3 %copy-start = (bf16[4,3,64]{2,0,1:T(4,128)(2,1)S(1)}, bf16[4,3,64]{2,0,1:T(4,128)(2,1)}, u32[]{:S(2)}) copy-start(bf16[4,3,64]{2,0,1:T(4,128)(2,1)} %param.23) | copy-start | bytes 4612

commit v2 on v0

--- a/solution.py
+++ b/solution.py
@@ -281,6 +281,429 @@
     )(x)
 
 
+SLOT = (0, 3, 1, 2)
+HALF = 64
+GROUPS = 4
+
+
+def iota(shape, dim):
+    return lax.broadcasted_iota(jnp.int32, shape, dim)
+
+
+def weave(w_in, w_mid, w_out, bias, we, wm, wo, bi):
+    feat = w_in.shape[2]
+    wide = feat * len(SLOT)
+    row, lane = iota((wide, wide), 0), iota((wide, wide), 1)
+    at, ch = lax.rem(row, HALF), row // HALF
+    slot = lane // feat
+    pos = jnp.where(slot == 1, 3, jnp.where(slot == 0, 0, slot - 1))
+    taps = w_in[...].astype(F32)
+    for par in range(2):
+        turned = lax.rem(at + (1 if par == 0 else HALF - 1), HALF)
+        tap = lax.rem(turned, 4)
+        base = jnp.zeros((wide, wide), F32)
+        for c in range(3):
+            for t in range(4):
+                line = jnp.concatenate([taps[c, t : t + 1, :]] * len(SLOT), axis=1)
+                base = jnp.where((ch == c) & (tap == t), line, base)
+        for g in range(GROUPS):
+            we[par * GROUPS + g] = jnp.where(turned // 4 == 4 * g + pos, base, 0.0).astype(BF16)
+    zero = jnp.zeros((feat, feat), F32)
+    mid = [w_mid[j].astype(F32) for j in range(3)]
+
+    def block(came, goes):
+        j = came - goes + 1
+        return mid[j] if 0 <= j < 3 else zero
+
+    for n, came in enumerate(SLOT):
+        blocks = [block(came, goes) for goes in SLOT]
+        wm[0, n * feat : (n + 1) * feat, :] = jnp.concatenate(blocks, axis=1).astype(BF16)
+    for n in range(4):
+        blocks = [zero] * 4
+        blocks[n ^ 1] = mid[2 if n % 2 == 0 else 0]
+        wm[1, n * feat : (n + 1) * feat, :] = jnp.concatenate(blocks, axis=1).astype(BF16)
+
+    def sample(shape):
+        col = iota(shape, 1)
+        m = lax.rem(col, HALF)
+        edge = jnp.where(m == HALF - 1, -1, jnp.where(m == 0, HALF, -4 * HALF))
+        return jnp.where(col >= 2 * HALF, edge, m)
+
+    near, far = sample((4, wide)), sample((feat, wide))
+    for par in range(2):
+        pick = jnp.where(lax.rem(near - 2 * par + 1 + 8 * HALF, 4) == iota((4, wide), 0), 1.0, 0.0).astype(BF16)
+        base = lax.dot_general(w_out[...], pick, (((0,), (0,)), ((), ())), preferred_element_type=F32)
+        for g in range(GROUPS):
+            for n, i in enumerate(SLOT):
+                d = far - 4 * (4 * g + i) - 2 * par + 1
+                at = ((par * GROUPS + g) * len(SLOT) + n) * feat
+                wo[at : at + feat, :] = jnp.where((d >= 0) & (d < 4), base, 0.0).astype(BF16)
+    bi[...] = jnp.concatenate([bias[...]] * len(SLOT), axis=1)
+
+
+def layers(zs, hs, gs, ys, we, wm, wo, bi):
+    b0, b1 = bi[0:1, :], bi[1:2, :]
+    rows, wide = zs.shape[1:]
+    blocks = ys.shape[0] - 2
+    per, half = rows // blocks, wide // 2
+    for par in range(2):
+        for g in range(GROUPS):
+            h = jnp.dot(zs[par], we[par * GROUPS + g], preferred_element_type=F32)
+            h = jnp.maximum(h + b0, 0.0).astype(BF16)
+            for b in range(blocks):
+                at = per + (b * GROUPS + g) * per
+                hs[par, at : at + per, :] = h[b * per : (b + 1) * per]
+    low = iota((rows, half), 1) < half // 2
+    for r in range(per, per + GROUPS * rows, rows):
+        edge = [jnp.where(low, hs[par, r + per : r + per + rows, :half], hs[par, r - per : r - per + rows, :half]) for par in range(2)]
+        edge = jnp.dot(jnp.concatenate(edge, axis=1), wm[1], preferred_element_type=F32)
+        for par in range(2):
+            g = jnp.dot(hs[par, r : r + rows, :], wm[0], preferred_element_type=F32)
+            ends = g[:, :half] + edge[:, par * half : (par + 1) * half]
+            g = [jnp.maximum(ends + b1[:, :half], 0.0), jnp.maximum(g[:, half:] + b1[:, half:], 0.0)]
+            for n in range(rows // per):
+                b, q = divmod(r // per - 1 + n, GROUPS)
+                for i in range(2):
+                    col = (par * GROUPS + q) * wide + i * half
+                    gs[b * per : (b + 1) * per, col : col + half] = g[i][n * per : (n + 1) * per].astype(BF16)
+    y = jnp.dot(gs[...], wo[...], preferred_element_type=F32)
+    ys[1 : 1 + blocks] = y.reshape(blocks, per, wide)
+
+
+def patch_kernel(sizes, lags, order, tallies, pace, guess, mixtures, *refs):
+    given, out = refs[:8], refs[8]
+    (gbuf, mbuf, sendx, recvx, sendm, recvm, backs, backr, sende, recve) = refs[9:19]
+    (xs, ps, mx, rolled, mf, member, zs, hs, gs, ys) = refs[19:29]
+    ta, tb, held = refs[29:33], refs[33:37], refs[37:45]
+    load_sem, ssem, rsem = refs[45:]
+    n_shot, n_line, n_tm = sizes
+    count = math.prod(sizes)
+    axes = [lax.axis_index(a) for a in AXES]
+    turns = [[axes[i]] + [lax.rem(axes[i] + d, n) for d in range(1, n)] for i, n in enumerate(sizes)]
+    at_shot, at_line, at_tm = axes
+
+    def number(s, l, t):
+        return (s * n_line + l) * n_tm + t
+
+    def device(s, l, t):
+        return {"shot": s, "line": l, "tm": t}
+
+    me = number(*axes)
+    peers = [(s, l, t) for s in turns[0] for l in turns[1] for t in turns[2]][1:]
+    shots = n_shot
+    n_mix = mixtures.shape[0]
+    run = shots // n_mix
+    recv_n, tl = guess.shape[1:]
+    lc = recv_n // count
+    tile = 2 * HALF
+    blocks = tl * n_tm // HALF
+    each = tl // HALF
+    back_kind = 2 + ITERS * n_line
+
+    barrier = pltpu.get_barrier_semaphore()
+    for p in peers:
+        pl.semaphore_signal(barrier, inc=1, device_id=device(*p), device_id_type=pl.DeviceIdType.MESH)
+    pairs = [(guess.at[0], gbuf), (mixtures, mbuf)] + list(zip(given, held))
+    loads = [pltpu.make_async_copy(a, b, load_sem.at[i]) for i, (a, b) in enumerate(pairs)]
+    for copy in loads:
+        copy.start()
+
+    def link(which, src, dst, to, came):
+        return pltpu.make_async_remote_copy(
+            src_ref=src,
+            dst_ref=dst,
+            send_sem=ssem.at[which, number(*to)],
+            recv_sem=rsem.at[which, came],
+            device_id=device(*to),
+            device_id_type=pl.DeviceIdType.MESH,
+        )
+
+    row, col = iota((recv_n, recv_n), 0), iota((recv_n, recv_n), 1)
+    perm = jnp.where(col == lax.rem(row, lc) * count + row // lc, 1.0, 0.0).astype(BF16)
+    loads[0].wait()
+    v = jnp.dot(perm, gbuf[...], preferred_element_type=F32)
+    for k in range(count):
+        part = v[k * lc : (k + 1) * lc]
+        sendx[k] = jnp.concatenate([part[:, : tl // 2], part[:, tl // 2 :]], axis=0).astype(BF16)
+    pl.semaphore_wait(barrier, count - 1)
+    for p in peers:
+        link(0, sendx.at[number(*p)], recvx.at[me], p, me).start()
+
+    loads[1].wait()
+    other = (at_shot, n_line - 1 - at_line, at_tm)
+    row, col = iota((2 * lc, recv_n), 0), iota((2 * lc, recv_n), 1)
+    wanted = jnp.where(row < lc, me, number(*other))
+    pick = jnp.where(col == lax.rem(row, lc) * count + wanted, 1.0, 0.0).astype(BF16)
+    picked = [jnp.dot(pick, mbuf[g], preferred_element_type=F32) for g in range(n_mix)]
+    sendm[...] = jnp.concatenate([p[lc:] for p in picked], axis=0).astype(BF16)
+    link(1, sendm, recvm.at[at_line], other, me).start()
+    recvm[at_line] = jnp.concatenate([p[:lc] for p in picked], axis=0).astype(BF16)
+    recvx[me] = sendx[me]
+
+    for copy in loads[2:]:
+        copy.wait()
+    weave(*held[:4], *ta)
+    weave(*held[4:], *tb)
+    edges = hs.shape[1] - (GROUPS * blocks + 1) * (hs.shape[1] // (GROUPS * blocks + 2))
+    hs[:, :edges] = jnp.zeros_like(hs[:, :edges])
+    hs[:, hs.shape[1] - edges :] = jnp.zeros_like(hs[:, :edges])
+    for ref in (ys, rolled, mf, xs):
+        ref[0] = jnp.zeros_like(ref[0])
+        ref[ref.shape[0] - 1] = jnp.zeros_like(ref[0])
+    for ref, at in ((rolled, 1), (mf, blocks)):
+        ref[at] = jnp.zeros_like(ref[at])
+    sec = []
+    for rows in ((lc, tile), (count, tile)):
+        if rows[0] == lc:
+            q = iota(rows, 0) * count + me
+        else:
+            q = lax.rem(iota(rows, 1), lc) * count + iota(rows, 0)
+        edge, at, size = jnp.int32(0), jnp.zeros(rows, jnp.int32), jnp.zeros(rows, jnp.int32)
+        for p in range(tallies.shape[0]):
+            at = jnp.where(q >= edge, p, at)
+            size = jnp.where(q >= edge, tallies[p], size)
+            edge = edge + tallies[p]
+        sec.append((at, size))
+    scale = 1.0 / (sec[0][1] * (shots * tl * n_tm)).astype(F32)
+    for k in range(count):
+        member[k] = jnp.where(sec[0][0] == sec[1][0][k : k + 1, :], scale, 0.0)
+
+    lane = iota((lc, tile), 1)
+    low = lane < HALF
+    inner = lax.rem(lane, HALF)
+
+    def unfold(v):
+        turned = pltpu.roll(v, HALF, 1)
+        return jnp.where(low, v, turned), jnp.where(low, turned, v)
+
+    for p in peers:
+        link(0, sendx.at[number(*p)], recvx.at[number(*p)], p, number(*p)).wait_recv()
+    for p in range(count):
+        s, l, t = p // (n_line * n_tm), p // n_tm % n_line, p % n_tm
+        v = recvx[p].astype(F32)
+        for j in range(tl // tile):
+            h, c = divmod(j * tile, tl // 2)
+            two = unfold(v[h * lc : (h + 1) * lc, c : c + tile])
+            for n in range(2):
+                xs[1 + l, t * each + 2 * j + n, s] = two[n]
+    link(1, sendm, recvm.at[n_line - 1 - at_line], other, number(*other)).wait_recv()
+    for l in range(n_line):
+        v = recvm[l].astype(F32)
+        for g in range(n_mix):
+            for j in range(blocks // 2):
+                two = unfold(v[g * lc : (g + 1) * lc, j * tile : (j + 1) * tile])
+                for n in range(2):
+                    mx[2 * j + n, g * n_line + l] = two[n]
+
+    cube = (shots, lc, tile)
+    per = shots * lc
+    clow = iota(cube, 2) < HALF
+    line_of = iota(cube, 1)
+    spot = lax.rem(iota((per, tile), 1), HALF)
+    wide_spot = lax.rem(iota((per, 2 * tile), 1), HALF)
+    early = spot < HALF // 2
+    one = jnp.zeros((1, lc, tile), F32)
+    nothing = jnp.zeros((per, 2 * tile), F32)
+
+    def widen(make):
+        ahead_of = [nothing, make(0)]
+        for b in range(blocks):
+            ahead_of.append(make(b + 1) if b + 1 < blocks else nothing)
+            before, here, after = ahead_of[b : b + 3]
+            zs[0, b * per : (b + 1) * per, :] = jnp.where(wide_spot == HALF - 1, before, here).astype(BF16)
+            zs[1, b * per : (b + 1) * per, :] = jnp.where(wide_spot == 0, after, here).astype(BF16)
+
+    def beside(before, here, after):
+        both = jnp.where(clow, before, here)
+        return jnp.concatenate([both.reshape(per, tile), after.reshape(per, tile)], axis=1)
+
+    def change(b):
+        return ys[b + 1, :, :tile] + jnp.where(early, ys[b, :, tile:], ys[b + 2, :, tile:])
+
+    group = []
+    for s in range(shots):
+        found = jnp.int32(0)
+        for k in range(shots):
+            found = jnp.where(order[k] == s, k // run, found)
+        group.append(found)
+    rest = [lax.rem(lags[s], HALF) for s in range(shots)]
+    far = [lags[s] // HALF for s in range(shots)]
+
+    def over_lines(it, l):
+        def make(b):
+            x = xs[1 + l, b]
+            before = jnp.where(line_of == lc - 1, xs[l, b], x)
+            after = jnp.where(line_of == 0, xs[2 + l, b], x)
+            return beside(pltpu.roll(before, 1, 1), x, pltpu.roll(after, lc - 1, 1))
+
+        widen(make)
+        layers(zs, hs, gs, ys, *ta)
+        energy = jnp.zeros((lc, tile), F32)
+        for b in range(blocks):
+            x = (xs[1 + l, b] + change(b).reshape(cube)).astype(BF16).astype(F32)
+            ps[l, b] = x
+            energy = energy + jnp.sum(x * x, axis=0)
+        energy = 0.5 * jnp.sum(energy, axis=1, keepdims=True)
+        mine = jnp.sum(jnp.where(lane == iota((lc, tile), 0), energy, 0.0), axis=0, keepdims=True)
+        at = it * n_line + l
+        sende[at] = mine
+        recve[at, me] = mine
+        for p in peers:
+            link(2 + at, sende.at[at], recve.at[at, me], p, me).start()
+
+    def over_shots(it, l):
+        at = it * n_line + l
+        for p in peers:
+            link(2 + at, sende.at[at], recve.at[at, number(*p)], p, number(*p)).wait_recv()
+        total = jnp.zeros((lc, tile), F32)
+        for k in range(count):
+            total = total + member[k] * recve[at, k]
+        mean = jnp.sum(total, axis=1, keepdims=True)
+        rms = jnp.broadcast_to(jnp.sqrt(mean + EPSILON), (lc, tile)).reshape(1, lc, tile)
+        inv = 1.0 / rms
+
+        def make(b):
+            x = (ps[l, b] * inv).astype(BF16).astype(F32)
+            return beside(jnp.concatenate([one, x[: shots - 1]], axis=0), x, jnp.concatenate([x[1:], one], axis=0))
+
+        widen(make)
+        layers(zs, hs, gs, ys, *tb)
+        for b in range(blocks):
+            x = (ps[l, b] + rms * change(b).reshape(cube)).astype(BF16).astype(F32)
+            ps[l, b] = x
+            for s in range(shots):
+                rolled[b + 2, s] = pltpu.roll(x[s], rest[s], 1)
+        for g in range(n_mix):
+            acc = -mx[:, g * n_line + l]
+            for i in range(run):
+                s = order[g * run + i]
+                lag = lags[s]
+                a = 2 - lag // HALF
+                near, late = rolled[pl.ds(a, blocks), s], rolled[pl.ds(a - 1, blocks), s]
+                acc = acc + jnp.where((inner >= lax.rem(lag, HALF))[None], near, late)
+            mf[:blocks, g] = acc
+        for s in range(shots):
+            m = mf[:, group[s]]
+            rolled[: blocks + 2, s] = pltpu.roll(m, lax.rem(tile - rest[s], tile), 2)
+        for s in range(shots):
+            near, late = rolled[pl.ds(far[s], blocks), s], rolled[pl.ds(far[s] + 1, blocks), s]
+            back = jnp.where((inner < HALF - rest[s])[None], near, late)
+            xs[1 + l, :, s] = (ps[l, :, s] - pace[it] * back).astype(BF16).astype(F32)
+        rolled[:2] = jnp.zeros_like(rolled[:2])
+
+        @pl.when(it == ITERS - 1)
+        def _():
+            for s in range(n_shot):
+                for t in range(n_tm):
+                    tiles = []
+                    for j in range(tl // tile):
+                        b = t * each + 2 * j
+                        tiles.append(jnp.where(low, xs[1 + l, b, s], xs[1 + l, b + 1, s]))
+                    n = len(tiles) // 2
+                    halves = [jnp.concatenate(tiles[:n], axis=1), jnp.concatenate(tiles[n:], axis=1)]
+                    backs[number(s, l, t)] = jnp.concatenate(halves, axis=0).astype(BF16)
+            own = (at_shot, l, at_tm)
+            for s in turns[0]:
+                for t in turns[2]:
+                    if s is at_shot and t is at_tm:
+                        continue
+                    link(back_kind, backs.at[number(s, l, t)], backr.at[me], (s, l, t), me).start()
+
+            @pl.when(l != at_line)
+            def _():
+                link(back_kind, backs.at[number(*own)], backr.at[me], own, me).start()
+
+    def iterate(it, carry):
+        def lines(l, carry):
+            over_lines(it, l)
+            return carry
+
+        def stations(l, carry):
+            over_shots(it, l)
+            return carry
+
+        lax.fori_loop(0, n_line, lines, 0)
+        lax.fori_loop(0, n_line, stations, 0)
+        return carry
+
+    lax.fori_loop(0, ITERS, iterate, 0)
+
+    backr[me] = backs[me]
+    row, col = iota((recv_n, recv_n), 0), iota((recv_n, recv_n), 1)
+    perm = jnp.where(row == lax.rem(col, lc) * count + col // lc, 1.0, 0.0).astype(BF16)
+    for p in peers:
+        link(back_kind, backs.at[number(*p)], backr.at[number(*p)], p, number(*p)).wait_recv()
+    v = []
+    for k in range(count):
+        part = backr[k].astype(F32)
+        v.append(jnp.concatenate([part[:lc], part[lc:]], axis=1))
+    v = jnp.concatenate(v, axis=0).astype(BF16)
+    out[0] = jnp.dot(perm, v, preferred_element_type=F32).astype(BF16)
+    link(1, sendm, recvm.at[at_line], other, me).wait_send()
+    for p in peers:
+        link(0, sendx.at[number(*p)], recvx.at[me], p, me).wait_send()
+        for at in range(ITERS * n_line):
+            link(2 + at, sende.at[at], recve.at[at, me], p, me).wait_send()
+        link(back_kind, backs.at[number(*p)], backr.at[me], p, me).wait_send()
+
+
+def patch(guess, mixtures, lags, order, tallies, wa, wb, pace, sizes):
+    count = math.prod(sizes)
+    n_shot, n_line, n_tm = sizes
+    recv, tl = guess.shape[1:]
+    n_mix, nt = mixtures.shape[0], mixtures.shape[2]
+    lc, tile = recv // count, 2 * HALF
+    blocks = nt // HALF
+    per, feat = n_shot * lc, wa[0].shape[2]
+    wide = feat * len(SLOT)
+    rows = blocks * per
+    weights = [w.transpose(1, 0, 2) if i == 0 else w for part in (wa, wb) for i, w in enumerate(part)]
+    v, s, h = (pl.BlockSpec(memory_space=m) for m in (pltpu.VMEM, pltpu.SMEM, pl.ANY))
+    slab = pltpu.VMEM((count, 2 * lc, tl // 2), BF16)
+    woven = [
+        pltpu.VMEM((2 * GROUPS, wide, wide), BF16),
+        pltpu.VMEM((2, wide, wide), BF16),
+        pltpu.VMEM((2 * GROUPS * wide, wide), BF16),
+        pltpu.VMEM((2, wide), F32),
+    ]
+    kinds = 3 + ITERS * n_line
+    return pl.pallas_call(
+        functools.partial(patch_kernel, sizes),
+        out_shape=jax.ShapeDtypeStruct(guess.shape, BF16),
+        in_specs=[s] * 4 + [h] * 10,
+        out_specs=v,
+        scratch_shapes=[
+            pltpu.VMEM((recv, tl), BF16),
+            pltpu.VMEM(mixtures.shape, BF16),
+            slab,
+            slab,
+            pltpu.VMEM((n_mix * lc, nt), BF16),
+            pltpu.VMEM((n_line, n_mix * lc, nt), BF16),
+            slab,
+            slab,
+            pltpu.VMEM((ITERS * n_line, 1, tile), F32),
+            pltpu.VMEM((ITERS * n_line, count, 1, tile), F32),
+            pltpu.VMEM((n_line + 2, blocks, n_shot, lc, tile), F32),
+            pltpu.VMEM((n_line, blocks, n_shot, lc, tile), F32),
+            pltpu.VMEM((blocks, n_mix * n_line, lc, tile), F32),
+            pltpu.VMEM((blocks + 2, n_shot, lc, tile), F32),
+            pltpu.VMEM((blocks + 2, n_mix, lc, tile), F32),
+            pltpu.VMEM((count, lc, tile), F32),
+            pltpu.VMEM((2, rows, wide), BF16),
+            pltpu.VMEM((2, GROUPS * rows + 2 * per, wide), BF16),
+            pltpu.VMEM((rows, 2 * GROUPS * wide), BF16),
+            pltpu.VMEM((blocks + 2, per, wide), F32),
+            *woven,
+            *woven,
+            *[pltpu.VMEM(w.shape, w.dtype) for w in weights],
+            pltpu.SemaphoreType.DMA((2 + len(weights),)),
+            pltpu.SemaphoreType.DMA((kinds, count)),
+            pltpu.SemaphoreType.DMA((kinds, count)),
+        ],
+        compiler_params=pltpu.CompilerParams(vmem_limit_bytes=56 * 2**20, collective_id=1, has_side_effects=True),
+    )(lags, order, tallies, pace, guess, mixtures, *weights)
+
+
 def per_device(guess, mixtures, lags, order, tallies, e1, m1, x1, b1, e2, m2, x2, b2, pace):
     sh, recv, tl = guess.shape
     n_shot, n_line, n_tm = (lax.axis_size(a) for a in AXES)
@@ -295,6 +718,13 @@
     lanes1, lanes2 = 2 * s1 * r1, 2 * shots * r2
     sources = n_shot if whole else 1
     i32 = functools.partial(jnp.arange, dtype=jnp.int32)
+    n_mix, feat = mixtures.shape[0], e1.shape[2]
+    square = sh == 1 and kp == 1 and n_line == 2 and shots % n_mix == 0 and feat == HALF
+    square = square and lh == C and tl % (4 * HALF) == 0 and n_mix * lh % 16 == 0
+    square = square and lines == parts and 2 * (n_mix // n_line) == n_line
+    if square:
+        sizes = (n_shot, n_line, n_tm)
+        return patch(guess, mixtures, lags, order, tallies, (e1, m1, x1, b1), (e2, m2, x2, b2), pace, sizes)
 
     at_shot = lax.axis_index("shot")
     n_mix, run = mixtures.shape[0], nt // C

time: 122 us -> 48.4 us (0.40)
  the two profiles are of different devices: /device:TPU:0 before, /device:TPU:7 now
where the time goes in v2:
time: 48.4 us; the launch traced here: 48.2 us
  Pallas kernels  46.7 us (96%)
  local copies, waits for them, and re-layouts  1.57 us (3%)
    pallas_call x1, Pallas kernels, patch(): pl.pallas_call(functools.partial(patch_kernel, sizes), out_shape=jax.Shap...  46.7 us
    unnamed x1, local copies, waits for them, and re-layouts  1.57 us

profile of v2, /device:TPU:7, one launch (start us, length us, event | category | flops | bytes accessed | tf_op | source)
XLA Modules:
  0.0 48.2 jit_solution(12523082693708724633)
XLA Ops:
  0.0 46.7 %shard_map.136 = bf16[1,128,512]{2,1,0:T(8,128)(2,1)} custom-call(s32[4]{0:T(128)} %lags.1, s32[4]{0:T(128)} %order.1, s32[8]{0:T(128)} %tallies.1, f32[2]{0:T(128)} %pace.1, bf16[1,128,512]{2,1,0:T(8,128)(2,1)} %guess.1, bf16[2,128,1024]{2,1,0:T(8,128)(2,1)} %mixtures.1, bf16[3,4,64]{2,1,0:T(4,128)(2,1)} %bitcast.2, bf16[3,64,64]{2,1,0:T(8,128)(2,1)} %refs_1_.1, ...), custom_call_target="tpu_custom_call" | custom-call | tf_op jit(solution)/shard_map/pallas_call | solution.py:670
  46.7 1.6 %copy.16 = bf16[1,128,512]{2,1,0:T(8,128)(2,1)} copy(bf16[1,128,512]{2,1,0:T(8,128)(2,1)} %shard_map.136) | data formatting | bytes 262144

commit v3 on v2

--- a/solution.py
+++ b/solution.py
@@ -366,8 +366,10 @@
                 for i in range(2):
                     col = (par * GROUPS + q) * wide + i * half
                     gs[b * per : (b + 1) * per, col : col + half] = g[i][n * per : (n + 1) * per].astype(BF16)
-    y = jnp.dot(gs[...], wo[...], preferred_element_type=F32)
-    ys[1 : 1 + blocks] = y.reshape(blocks, per, wide)
+    part = blocks // 4
+    for b in range(0, blocks, part):
+        y = jnp.dot(gs[b * per : (b + part) * per, :], wo[...], preferred_element_type=F32)
+        ys[1 + b : 1 + b + part] = y.reshape(part, per, wide)
 
 
 def patch_kernel(sizes, lags, order, tallies, pace, guess, mixtures, *refs):

time: 48.4 us -> 42.1 us (0.87)
  Pallas kernels: 46.7 us -> 40.3 us
    pallas_call x1, Pallas kernels: 46.7 us -> 40.3 us  [patch(): pl.pallas_call(functools.partial(patch_kernel, sizes), out_shape=jax.Shap...]
where the time goes in v3:
time: 42.1 us; the launch traced here: 41.9 us
  Pallas kernels  40.3 us (96%)
  local copies, waits for them, and re-layouts  1.57 us (4%)
    pallas_call x1, Pallas kernels, patch(): pl.pallas_call(functools.partial(patch_kernel, sizes), out_shape=jax.Shap...  40.3 us
    unnamed x1, local copies, waits for them, and re-layouts  1.57 us

profile of v3, /device:TPU:7, one launch (start us, length us, event | category | flops | bytes accessed | tf_op | source)
XLA Modules:
  0.0 41.9 jit_solution(14032861185081545165)
XLA Ops:
  0.0 40.3 %shard_map.136 = bf16[1,128,512]{2,1,0:T(8,128)(2,1)} custom-call(s32[4]{0:T(128)} %lags.1, s32[4]{0:T(128)} %order.1, s32[8]{0:T(128)} %tallies.1, f32[2]{0:T(128)} %pace.1, bf16[1,128,512]{2,1,0:T(8,128)(2,1)} %guess.1, bf16[2,128,1024]{2,1,0:T(8,128)(2,1)} %mixtures.1, bf16[3,4,64]{2,1,0:T(4,128)(2,1)} %bitcast.2, bf16[3,64,64]{2,1,0:T(8,128)(2,1)} %refs_1_.1, ...), custom_call_target="tpu_custom_call" | custom-call | tf_op jit(solution)/shard_map/pallas_call | solution.py:672
  40.3 1.6 %copy.16 = bf16[1,128,512]{2,1,0:T(8,128)(2,1)} copy(bf16[1,128,512]{2,1,0:T(8,128)(2,1)} %shard_map.136) | data formatting | bytes 262144

commit v4 on v3

--- a/solution.py
+++ b/solution.py
@@ -341,15 +341,19 @@
     bi[...] = jnp.concatenate([bias[...]] * len(SLOT), axis=1)
 
 
-def layers(zs, hs, gs, ys, we, wm, wo, bi):
-    b0, b1 = bi[0:1, :], bi[1:2, :]
+def rectified(h, bias):
+    cubes = h.reshape(h.shape[0] // bias.shape[0], bias.shape[0], h.shape[1])
+    return jnp.maximum(cubes + bias[None], 0.0).reshape(h.shape)
+
+
+def layers(zs, hs, gs, ys, we, wm, wo, b0, b1):
     rows, wide = zs.shape[1:]
     blocks = ys.shape[0] - 2
     per, half = rows // blocks, wide // 2
     for par in range(2):
         for g in range(GROUPS):
             h = jnp.dot(zs[par], we[par * GROUPS + g], preferred_element_type=F32)
-            h = jnp.maximum(h + b0, 0.0).astype(BF16)
+            h = rectified(h, b0).astype(BF16)
             for b in range(blocks):
                 at = per + (b * GROUPS + g) * per
                 hs[par, at : at + per, :] = h[b * per : (b + 1) * per]
@@ -360,7 +364,7 @@
         for par in range(2):
             g = jnp.dot(hs[par, r : r + rows, :], wm[0], preferred_element_type=F32)
             ends = g[:, :half] + edge[:, par * half : (par + 1) * half]
-            g = [jnp.maximum(ends + b1[:, :half], 0.0), jnp.maximum(g[:, half:] + b1[:, half:], 0.0)]
+            g = [rectified(ends, b1[:, :half]), rectified(g[:, half:], b1[:, half:])]
             for n in range(rows // per):
                 b, q = divmod(r // per - 1 + n, GROUPS)
                 for i in range(2):
@@ -372,12 +376,14 @@
         ys[1 + b : 1 + b + part] = y.reshape(part, per, wide)
 
 
-def patch_kernel(sizes, lags, order, tallies, pace, guess, mixtures, *refs):
+def patch_kernel(sizes, *refs):
+    scalars, (guess, mixtures), refs = refs[:4], refs[4:6], refs[6:]
+    lags, order, tallies, pace = refs[45:49]
     given, out = refs[:8], refs[8]
     (gbuf, mbuf, sendx, recvx, sendm, recvm, backs, backr, sende, recve) = refs[9:19]
     (xs, ps, mx, rolled, mf, member, zs, hs, gs, ys) = refs[19:29]
     ta, tb, held = refs[29:33], refs[33:37], refs[37:45]
-    load_sem, ssem, rsem = refs[45:]
+    load_sem, ssem, rsem = refs[49:]
     n_shot, n_line, n_tm = sizes
     count = math.prod(sizes)
     axes = [lax.axis_index(a) for a in AXES]
@@ -405,7 +411,7 @@
     barrier = pltpu.get_barrier_semaphore()
     for p in peers:
         pl.semaphore_signal(barrier, inc=1, device_id=device(*p), device_id_type=pl.DeviceIdType.MESH)
-    pairs = [(guess.at[0], gbuf), (mixtures, mbuf)] + list(zip(given, held))
+    pairs = [(guess.at[0], gbuf), (mixtures, mbuf)] + list(zip(given, held)) + list(zip(scalars, refs[45:49]))
     loads = [pltpu.make_async_copy(a, b, load_sem.at[i]) for i, (a, b) in enumerate(pairs)]
     for copy in loads:
         copy.start()
@@ -539,7 +545,8 @@
             return beside(pltpu.roll(before, 1, 1), x, pltpu.roll(after, lc - 1, 1))
 
         widen(make)
-        layers(zs, hs, gs, ys, *ta)
+        biases = [jnp.broadcast_to(ta[3][i : i + 1, :], (lc, 2 * tile)) for i in range(2)]
+        layers(zs, hs, gs, ys, *ta[:3], *biases)
         energy = jnp.zeros((lc, tile), F32)
         for b in range(blocks):
             x = (xs[1 + l, b] + change(b).reshape(cube)).astype(BF16).astype(F32)
@@ -554,6 +561,11 @@
             link(2 + at, sende.at[at], recve.at[at, me], p, me).start()
 
     def over_shots(it, l):
+        def make(b):
+            x = ps[l, b]
+            return beside(jnp.concatenate([one, x[: shots - 1]], axis=0), x, jnp.concatenate([x[1:], one], axis=0))
+
+        widen(make)
         at = it * n_line + l
         for p in peers:
             link(2 + at, sende.at[at], recve.at[at, number(*p)], p, number(*p)).wait_recv()
@@ -561,17 +573,11 @@
         for k in range(count):
             total = total + member[k] * recve[at, k]
         mean = jnp.sum(total, axis=1, keepdims=True)
-        rms = jnp.broadcast_to(jnp.sqrt(mean + EPSILON), (lc, tile)).reshape(1, lc, tile)
-        inv = 1.0 / rms
-
-        def make(b):
-            x = (ps[l, b] * inv).astype(BF16).astype(F32)
-            return beside(jnp.concatenate([one, x[: shots - 1]], axis=0), x, jnp.concatenate([x[1:], one], axis=0))
-
-        widen(make)
-        layers(zs, hs, gs, ys, *tb)
+        rms = jnp.broadcast_to(jnp.sqrt(mean + EPSILON), (lc, 2 * tile))
+        biases = [rms * tb[3][i : i + 1, :] for i in range(2)]
+        layers(zs, hs, gs, ys, *tb[:3], *biases)
         for b in range(blocks):
-            x = (ps[l, b] + rms * change(b).reshape(cube)).astype(BF16).astype(F32)
+            x = (ps[l, b] + change(b).reshape(cube)).astype(BF16).astype(F32)
             ps[l, b] = x
             for s in range(shots):
                 rolled[b + 2, s] = pltpu.roll(x[s], rest[s], 1)
@@ -660,7 +666,7 @@
     wide = feat * len(SLOT)
     rows = blocks * per
     weights = [w.transpose(1, 0, 2) if i == 0 else w for part in (wa, wb) for i, w in enumerate(part)]
-    v, s, h = (pl.BlockSpec(memory_space=m) for m in (pltpu.VMEM, pltpu.SMEM, pl.ANY))
+    v, h = (pl.BlockSpec(memory_space=m) for m in (pltpu.VMEM, pl.ANY))
     slab = pltpu.VMEM((count, 2 * lc, tl // 2), BF16)
     woven = [
         pltpu.VMEM((2 * GROUPS, wide, wide), BF16),
@@ -671,8 +677,8 @@
     kinds = 3 + ITERS * n_line
     return pl.pallas_call(
         functools.partial(patch_kernel, sizes),
-        out_shape=jax.ShapeDtypeStruct(guess.shape, BF16),
-        in_specs=[s] * 4 + [h] * 10,
+        out_shape=pltpu.VMEM(guess.shape, BF16),
+        in_specs=[h] * 14,
         out_specs=v,
         scratch_shapes=[
             pltpu.VMEM((recv, tl), BF16),
@@ -698,7 +704,8 @@
             *woven,
             *woven,
             *[pltpu.VMEM(w.shape, w.dtype) for w in weights],
-            pltpu.SemaphoreType.DMA((2 + len(weights),)),
+            *[pltpu.SMEM(w.shape, w.dtype) for w in (lags, order, tallies, pace)],
+            pltpu.SemaphoreType.DMA((6 + len(weights),)),
             pltpu.SemaphoreType.DMA((kinds, count)),
             pltpu.SemaphoreType.DMA((kinds, count)),
         ],

time: 42.1 us -> 39.5 us (0.938)
  Pallas kernels: 40.3 us -> 38.7 us
  local copies, waits for them, and re-layouts: 1.57 us -> 0.66 us
    pallas_call x1, Pallas kernels: 40.3 us -> 38.7 us  [patch(): pl.pallas_call(functools.partial(patch_kernel, sizes), out_shape=pltpu.VM...]
    unnamed x1, local copies, waits for them, and re-layouts: 1.57 us -> 0.66 us
where the time goes in v4:
time: 39.5 us; the launch traced here: 39.4 us
  Pallas kernels  38.7 us (98%)
  local copies, waits for them, and re-layouts  0.66 us (2%)
    pallas_call x1, Pallas kernels, patch(): pl.pallas_call(functools.partial(patch_kernel, sizes), out_shape=pltpu.VM...  38.7 us

profile of v4, /device:TPU:7, one launch (start us, length us, event | category | flops | bytes accessed | tf_op | source)
XLA Modules:
  0.0 39.4 jit_solution(17434226121920703149)
XLA Ops:
  0.0 38.7 %shard_map.136 = bf16[1,128,512]{2,1,0:T(8,128)(2,1)S(1)} custom-call(s32[4]{0:T(128)} %refs_0_.1, s32[4]{0:T(128)} %refs_1_.1, s32[8]{0:T(128)} %refs_2_.1, f32[2]{0:T(128)} %refs_3_.1, bf16[1,128,512]{2,1,0:T(8,128)(2,1)} %refs_4_.1, bf16[2,128,1024]{2,1,0:T(8,128)(2,1)} %refs_5_.1, bf16[3,4,64]{2,1,0:T(4,128)(2,1)} %bitcast.2, ...), custom_call_target="tpu_custom_call" | custom-call | tf_op jit(solution)/shard_map/pallas_call | solution.py:678
  38.7 0.7 %copy.16 = bf16[1,128,512]{2,1,0:T(8,128)(2,1)} copy(bf16[1,128,512]{2,1,0:T(8,128)(2,1)S(1)} %shard_map.136) | data formatting | bytes 262144

commit v5 on v4

--- a/solution.py
+++ b/solution.py
@@ -346,10 +346,8 @@
     return jnp.maximum(cubes + bias[None], 0.0).reshape(h.shape)
 
 
-def layers(zs, hs, gs, ys, we, wm, wo, b0, b1):
-    rows, wide = zs.shape[1:]
-    blocks = ys.shape[0] - 2
-    per, half = rows // blocks, wide // 2
+def enter(zs, hs, we, b0, blocks):
+    per = zs.shape[1] // blocks
     for par in range(2):
         for g in range(GROUPS):
             h = jnp.dot(zs[par], we[par * GROUPS + g], preferred_element_type=F32)
@@ -357,6 +355,28 @@
             for b in range(blocks):
                 at = per + (b * GROUPS + g) * per
                 hs[par, at : at + per, :] = h[b * per : (b + 1) * per]
+
+
+def prepare(zs, pre, we):
+    for par in range(2):
+        for g in range(GROUPS):
+            pre[par * GROUPS + g] = jnp.dot(zs[par], we[par * GROUPS + g], preferred_element_type=F32)
+
+
+def complete(pre, hs, b0, blocks):
+    per = pre.shape[1] // blocks
+    for b in range(blocks):
+        for par in range(2):
+            for g in range(GROUPS):
+                at = per + (b * GROUPS + g) * per
+                h = pre[par * GROUPS + g, b * per : (b + 1) * per, :]
+                hs[par, at : at + per, :] = rectified(h, b0).astype(BF16)
+
+
+def leave(hs, gs, ys, wm, wo, b1):
+    rows, wide = gs.shape[0], hs.shape[2]
+    blocks = ys.shape[0] - 2
+    per, half = rows // blocks, wide // 2
     low = iota((rows, half), 1) < half // 2
     for r in range(per, per + GROUPS * rows, rows):
         edge = [jnp.where(low, hs[par, r + per : r + per + rows, :half], hs[par, r - per : r - per + rows, :half]) for par in range(2)]
@@ -382,8 +402,9 @@
     given, out = refs[:8], refs[8]
     (gbuf, mbuf, sendx, recvx, sendm, recvm, backs, backr, sende, recve) = refs[9:19]
     (xs, ps, mx, rolled, mf, member, zs, hs, gs, ys) = refs[19:29]
+    pre = refs[49]
     ta, tb, held = refs[29:33], refs[33:37], refs[37:45]
-    load_sem, ssem, rsem = refs[49:]
+    load_sem, ssem, rsem = refs[50:]
     n_shot, n_line, n_tm = sizes
     count = math.prod(sizes)
     axes = [lax.axis_index(a) for a in AXES]
@@ -494,14 +515,16 @@
             two = unfold(v[h * lc : (h + 1) * lc, c : c + tile])
             for n in range(2):
                 xs[1 + l, t * each + 2 * j + n, s] = two[n]
-    link(1, sendm, recvm.at[n_line - 1 - at_line], other, number(*other)).wait_recv()
-    for l in range(n_line):
-        v = recvm[l].astype(F32)
-        for g in range(n_mix):
-            for j in range(blocks // 2):
-                two = unfold(v[g * lc : (g + 1) * lc, j * tile : (j + 1) * tile])
-                for n in range(2):
-                    mx[2 * j + n, g * n_line + l] = two[n]
+
+    def unfold_mixtures():
+        link(1, sendm, recvm.at[n_line - 1 - at_line], other, number(*other)).wait_recv()
+        for l in range(n_line):
+            v = recvm[l].astype(F32)
+            for g in range(n_mix):
+                for j in range(blocks // 2):
+                    two = unfold(v[g * lc : (g + 1) * lc, j * tile : (j + 1) * tile])
+                    for n in range(2):
+                        mx[2 * j + n, g * n_line + l] = two[n]
 
     cube = (shots, lc, tile)
     per = shots * lc
@@ -546,7 +569,8 @@
 
         widen(make)
         biases = [jnp.broadcast_to(ta[3][i : i + 1, :], (lc, 2 * tile)) for i in range(2)]
-        layers(zs, hs, gs, ys, *ta[:3], *biases)
+        enter(zs, hs, ta[0], biases[0], blocks)
+        leave(hs, gs, ys, *ta[1:3], biases[1])
         energy = jnp.zeros((lc, tile), F32)
         for b in range(blocks):
             x = (xs[1 + l, b] + change(b).reshape(cube)).astype(BF16).astype(F32)
@@ -560,12 +584,15 @@
         for p in peers:
             link(2 + at, sende.at[at], recve.at[at, me], p, me).start()
 
-    def over_shots(it, l):
+    def before_shots(l):
         def make(b):
             x = ps[l, b]
             return beside(jnp.concatenate([one, x[: shots - 1]], axis=0), x, jnp.concatenate([x[1:], one], axis=0))
 
         widen(make)
+        prepare(zs, pre.at[l], tb[0])
+
+    def over_shots(it, l):
         at = it * n_line + l
         for p in peers:
             link(2 + at, sende.at[at], recve.at[at, number(*p)], p, number(*p)).wait_recv()
@@ -575,7 +602,8 @@
         mean = jnp.sum(total, axis=1, keepdims=True)
         rms = jnp.broadcast_to(jnp.sqrt(mean + EPSILON), (lc, 2 * tile))
         biases = [rms * tb[3][i : i + 1, :] for i in range(2)]
-        layers(zs, hs, gs, ys, *tb[:3], *biases)
+        complete(pre.at[l], hs, biases[0], blocks)
+        leave(hs, gs, ys, *tb[1:3], biases[1])
         for b in range(blocks):
             x = (ps[l, b] + change(b).reshape(cube)).astype(BF16).astype(F32)
             ps[l, b] = x
@@ -630,7 +658,17 @@
             over_shots(it, l)
             return carry
 
+        def first(l, carry):
+            before_shots(l)
+            return carry
+
         lax.fori_loop(0, n_line, lines, 0)
+        lax.fori_loop(0, n_line, first, 0)
+
+        @pl.when(it == 0)
+        def _():
+            unfold_mixtures()
+
         lax.fori_loop(0, n_line, stations, 0)
         return carry
 
@@ -705,6 +743,7 @@
             *woven,
             *[pltpu.VMEM(w.shape, w.dtype) for w in weights],
             *[pltpu.SMEM(w.shape, w.dtype) for w in (lags, order, tallies, pace)],
+            pltpu.VMEM((n_line, 2 * GROUPS, rows, wide), F32),
             pltpu.SemaphoreType.DMA((6 + len(weights),)),
             pltpu.SemaphoreType.DMA((kinds, count)),
             pltpu.SemaphoreType.DMA((kinds, count)),

time: 39.5 us -> 38.7 us (0.980)
  Pallas kernels: 38.7 us -> 37.9 us
    pallas_call x1, Pallas kernels: 38.7 us -> 37.9 us  [patch(): pl.pallas_call(functools.partial(patch_kernel, sizes), out_shape=pltpu.VM...]
where the time goes in v5:
time: 38.7 us; the launch traced here: 38.6 us
  Pallas kernels  37.9 us (98%)
  local copies, waits for them, and re-layouts  0.66 us (2%)
    pallas_call x1, Pallas kernels, patch(): pl.pallas_call(functools.partial(patch_kernel, sizes), out_shape=pltpu.VM...  37.9 us

profile of v5, /device:TPU:7, one launch (start us, length us, event | category | flops | bytes accessed | tf_op | source)
XLA Modules:
  0.0 38.6 jit_solution(18421096666505676371)
XLA Ops:
  0.0 37.9 %shard_map.136 = bf16[1,128,512]{2,1,0:T(8,128)(2,1)S(1)} custom-call(s32[4]{0:T(128)} %refs_0_.1, s32[4]{0:T(128)} %refs_1_.1, s32[8]{0:T(128)} %refs_2_.1, f32[2]{0:T(128)} %refs_3_.1, bf16[1,128,512]{2,1,0:T(8,128)(2,1)} %refs_4_.1, bf16[2,128,1024]{2,1,0:T(8,128)(2,1)} %refs_5_.1, bf16[3,4,64]{2,1,0:T(4,128)(2,1)} %bitcast.2, ...), custom_call_target="tpu_custom_call" | custom-call | tf_op jit(solution)/shard_map/pallas_call | solution.py:716
  37.9 0.7 %copy.16 = bf16[1,128,512]{2,1,0:T(8,128)(2,1)} copy(bf16[1,128,512]{2,1,0:T(8,128)(2,1)S(1)} %shard_map.136) | data formatting | bytes 262144

commit v6 on v5

--- a/solution.py
+++ b/solution.py
@@ -357,32 +357,31 @@
                 hs[par, at : at + per, :] = h[b * per : (b + 1) * per]
 
 
-def prepare(zs, pre, we):
+def prepare(zs, pre, we, blocks):
+    per = zs.shape[1] // blocks
     for par in range(2):
         for g in range(GROUPS):
-            pre[par * GROUPS + g] = jnp.dot(zs[par], we[par * GROUPS + g], preferred_element_type=F32)
-
-
-def complete(pre, hs, b0, blocks):
-    per = pre.shape[1] // blocks
-    for b in range(blocks):
-        for par in range(2):
-            for g in range(GROUPS):
+            h = jnp.dot(zs[par], we[par * GROUPS + g], preferred_element_type=F32)
+            for b in range(blocks):
                 at = per + (b * GROUPS + g) * per
-                h = pre[par * GROUPS + g, b * per : (b + 1) * per, :]
-                hs[par, at : at + per, :] = rectified(h, b0).astype(BF16)
-
-
-def leave(hs, gs, ys, wm, wo, b1):
+                pre[par, at : at + per, :] = h[b * per : (b + 1) * per]
+
+
+def leave(hs, gs, ys, wm, wo, b1, b0=None):
     rows, wide = gs.shape[0], hs.shape[2]
     blocks = ys.shape[0] - 2
     per, half = rows // blocks, wide // 2
     low = iota((rows, half), 1) < half // 2
     for r in range(per, per + GROUPS * rows, rows):
         edge = [jnp.where(low, hs[par, r + per : r + per + rows, :half], hs[par, r - per : r - per + rows, :half]) for par in range(2)]
+        if b0 is not None:
+            edge = [rectified(e, b0[:, :half]).astype(BF16) for e in edge]
         edge = jnp.dot(jnp.concatenate(edge, axis=1), wm[1], preferred_element_type=F32)
         for par in range(2):
-            g = jnp.dot(hs[par, r : r + rows, :], wm[0], preferred_element_type=F32)
+            here = hs[par, r : r + rows, :]
+            if b0 is not None:
+                here = rectified(here, b0).astype(BF16)
+            g = jnp.dot(here, wm[0], preferred_element_type=F32)
             ends = g[:, :half] + edge[:, par * half : (par + 1) * half]
             g = [rectified(ends, b1[:, :half]), rectified(g[:, half:], b1[:, half:])]
             for n in range(rows // per):
@@ -476,6 +475,9 @@
     edges = hs.shape[1] - (GROUPS * blocks + 1) * (hs.shape[1] // (GROUPS * blocks + 2))
     hs[:, :edges] = jnp.zeros_like(hs[:, :edges])
     hs[:, hs.shape[1] - edges :] = jnp.zeros_like(hs[:, :edges])
+    silent = jnp.full((n_line, 2, edges, pre.shape[3]), -1e30, F32)
+    pre[:, :, :edges] = silent
+    pre[:, :, pre.shape[2] - edges :] = silent
     for ref in (ys, rolled, mf, xs):
         ref[0] = jnp.zeros_like(ref[0])
         ref[ref.shape[0] - 1] = jnp.zeros_like(ref[0])
@@ -590,7 +592,7 @@
             return beside(jnp.concatenate([one, x[: shots - 1]], axis=0), x, jnp.concatenate([x[1:], one], axis=0))
 
         widen(make)
-        prepare(zs, pre.at[l], tb[0])
+        prepare(zs, pre.at[l], tb[0], blocks)
 
     def over_shots(it, l):
         at = it * n_line + l
@@ -602,8 +604,7 @@
         mean = jnp.sum(total, axis=1, keepdims=True)
         rms = jnp.broadcast_to(jnp.sqrt(mean + EPSILON), (lc, 2 * tile))
         biases = [rms * tb[3][i : i + 1, :] for i in range(2)]
-        complete(pre.at[l], hs, biases[0], blocks)
-        leave(hs, gs, ys, *tb[1:3], biases[1])
+        leave(pre.at[l], gs, ys, *tb[1:3], biases[1], biases[0])
         for b in range(blocks):
             x = (ps[l, b] + change(b).reshape(cube)).astype(BF16).astype(F32)
             ps[l, b] = x
@@ -743,7 +744,7 @@
             *woven,
             *[pltpu.VMEM(w.shape, w.dtype) for w in weights],
             *[pltpu.SMEM(w.shape, w.dtype) for w in (lags, order, tallies, pace)],
-            pltpu.VMEM((n_line, 2 * GROUPS, rows, wide), F32),
+            pltpu.VMEM((n_line, 2, GROUPS * rows + 2 * per, wide), F32),
             pltpu.SemaphoreType.DMA((6 + len(weights),)),
             pltpu.SemaphoreType.DMA((kinds, count)),
             pltpu.SemaphoreType.DMA((kinds, count)),

time: 38.7 us -> 37.9 us (0.979)
  Pallas kernels: 37.9 us -> 37.1 us
    pallas_call x1, Pallas kernels: 37.9 us -> 37.1 us  [patch(): pl.pallas_call(functools.partial(patch_kernel, sizes), out_shape=pltpu.VM...]
where the time goes in v6:
time: 37.9 us; the launch traced here: 37.7 us
  Pallas kernels  37.1 us (98%)
  local copies, waits for them, and re-layouts  0.66 us (2%)
    pallas_call x1, Pallas kernels, patch(): pl.pallas_call(functools.partial(patch_kernel, sizes), out_shape=pltpu.VM...  37.1 us

profile of v6, /device:TPU:7, one launch (start us, length us, event | category | flops | bytes accessed | tf_op | source)
XLA Modules:
  0.0 37.7 jit_solution(14768382122624941847)
XLA Ops:
  0.0 37.1 %shard_map.136 = bf16[1,128,512]{2,1,0:T(8,128)(2,1)S(1)} custom-call(s32[4]{0:T(128)} %refs_0_.1, s32[4]{0:T(128)} %refs_1_.1, s32[8]{0:T(128)} %refs_2_.1, f32[2]{0:T(128)} %refs_3_.1, bf16[1,128,512]{2,1,0:T(8,128)(2,1)} %refs_4_.1, bf16[2,128,1024]{2,1,0:T(8,128)(2,1)} %refs_5_.1, bf16[3,4,64]{2,1,0:T(4,128)(2,1)} %bitcast.2, ...), custom_call_target="tpu_custom_call" | custom-call | tf_op jit(solution)/shard_map/pallas_call | solution.py:717
  37.1 0.7 %copy.16 = bf16[1,128,512]{2,1,0:T(8,128)(2,1)} copy(bf16[1,128,512]{2,1,0:T(8,128)(2,1)S(1)} %shard_map.136) | data formatting | bytes 262144

commit v7 on v6

--- a/solution.py
+++ b/solution.py
@@ -454,7 +454,7 @@
         part = v[k * lc : (k + 1) * lc]
         sendx[k] = jnp.concatenate([part[:, : tl // 2], part[:, tl // 2 :]], axis=0).astype(BF16)
     pl.semaphore_wait(barrier, count - 1)
-    for p in peers:
+    for p in peers[::-1]:
         link(0, sendx.at[number(*p)], recvx.at[me], p, me).start()
 
     loads[1].wait()
@@ -583,7 +583,7 @@
         at = it * n_line + l
         sende[at] = mine
         recve[at, me] = mine
-        for p in peers:
+        for p in peers[::-1]:
             link(2 + at, sende.at[at], recve.at[at, me], p, me).start()
 
     def before_shots(l):
@@ -678,6 +678,11 @@
     backr[me] = backs[me]
     row, col = iota((recv_n, recv_n), 0), iota((recv_n, recv_n), 1)
     perm = jnp.where(row == lax.rem(col, lc) * count + col // lc, 1.0, 0.0).astype(BF16)
+    link(1, sendm, recvm.at[at_line], other, me).wait_send()
+    for p in peers:
+        link(0, sendx.at[number(*p)], recvx.at[me], p, me).wait_send()
+        for at in range(ITERS * n_line):
+            link(2 + at, sende.at[at], recve.at[at, me], p, me).wait_send()
     for p in peers:
         link(back_kind, backs.at[number(*p)], backr.at[number(*p)], p, number(*p)).wait_recv()
     v = []
@@ -686,11 +691,7 @@
         v.append(jnp.concatenate([part[:lc], part[lc:]], axis=1))
     v = jnp.concatenate(v, axis=0).astype(BF16)
     out[0] = jnp.dot(perm, v, preferred_element_type=F32).astype(BF16)
-    link(1, sendm, recvm.at[at_line], other, me).wait_send()
     for p in peers:
-        link(0, sendx.at[number(*p)], recvx.at[me], p, me).wait_send()
-        for at in range(ITERS * n_line):
-            link(2 + at, sende.at[at], recve.at[at, me], p, me).wait_send()
         link(back_kind, backs.at[number(*p)], backr.at[me], p, me).wait_send()
 
 

time: 37.9 us -> 37.5 us (0.989)
  Pallas kernels: 37.1 us -> 36.7 us
    pallas_call x1, Pallas kernels: 37.1 us -> 36.7 us  [patch(): pl.pallas_call(functools.partial(patch_kernel, sizes), out_shape=pltpu.VM...]
where the time goes in v7:
time: 37.5 us; the launch traced here: 37.3 us
  Pallas kernels  36.7 us (98%)
  local copies, waits for them, and re-layouts  0.66 us (2%)
    pallas_call x1, Pallas kernels, patch(): pl.pallas_call(functools.partial(patch_kernel, sizes), out_shape=pltpu.VM...  36.7 us

profile of v7, /device:TPU:7, one launch (start us, length us, event | category | flops | bytes accessed | tf_op | source)
XLA Modules:
  0.0 37.3 jit_solution(1548499086171002404)
XLA Ops:
  0.0 36.7 %shard_map.136 = bf16[1,128,512]{2,1,0:T(8,128)(2,1)S(1)} custom-call(s32[4]{0:T(128)} %refs_0_.1, s32[4]{0:T(128)} %refs_1_.1, s32[8]{0:T(128)} %refs_2_.1, f32[2]{0:T(128)} %refs_3_.1, bf16[1,128,512]{2,1,0:T(8,128)(2,1)} %refs_4_.1, bf16[2,128,1024]{2,1,0:T(8,128)(2,1)} %refs_5_.1, bf16[3,4,64]{2,1,0:T(4,128)(2,1)} %bitcast.2, ...), custom_call_target="tpu_custom_call" | custom-call | tf_op jit(solution)/shard_map/pallas_call | solution.py:718
  36.7 0.7 %copy.16 = bf16[1,128,512]{2,1,0:T(8,128)(2,1)} copy(bf16[1,128,512]{2,1,0:T(8,128)(2,1)S(1)} %shard_map.136) | data formatting | bytes 262144

commit v8 on v7

--- a/solution.py
+++ b/solution.py
@@ -371,20 +371,21 @@
     rows, wide = gs.shape[0], hs.shape[2]
     blocks = ys.shape[0] - 2
     per, half = rows // blocks, wide // 2
-    low = iota((rows, half), 1) < half // 2
-    for r in range(per, per + GROUPS * rows, rows):
-        edge = [jnp.where(low, hs[par, r + per : r + per + rows, :half], hs[par, r - per : r - per + rows, :half]) for par in range(2)]
+    low = iota((2 * rows, half), 1) < half // 2
+    take = 2 * rows
+    for r in range(per, per + GROUPS * rows, take):
+        edge = [jnp.where(low, hs[par, r + per : r + per + take, :half], hs[par, r - per : r - per + take, :half]) for par in range(2)]
         if b0 is not None:
             edge = [rectified(e, b0[:, :half]).astype(BF16) for e in edge]
         edge = jnp.dot(jnp.concatenate(edge, axis=1), wm[1], preferred_element_type=F32)
         for par in range(2):
-            here = hs[par, r : r + rows, :]
+            here = hs[par, r : r + take, :]
             if b0 is not None:
                 here = rectified(here, b0).astype(BF16)
             g = jnp.dot(here, wm[0], preferred_element_type=F32)
             ends = g[:, :half] + edge[:, par * half : (par + 1) * half]
             g = [rectified(ends, b1[:, :half]), rectified(g[:, half:], b1[:, half:])]
-            for n in range(rows // per):
+            for n in range(take // per):
                 b, q = divmod(r // per - 1 + n, GROUPS)
                 for i in range(2):
                     col = (par * GROUPS + q) * wide + i * half
@@ -640,8 +641,8 @@
                     halves = [jnp.concatenate(tiles[:n], axis=1), jnp.concatenate(tiles[n:], axis=1)]
                     backs[number(s, l, t)] = jnp.concatenate(halves, axis=0).astype(BF16)
             own = (at_shot, l, at_tm)
-            for s in turns[0]:
-                for t in turns[2]:
+            for s in turns[0][::-1]:
+                for t in turns[2][::-1]:
                     if s is at_shot and t is at_tm:
                         continue
                     link(back_kind, backs.at[number(s, l, t)], backr.at[me], (s, l, t), me).start()

time: 37.5 us -> 37.5 us (level)
  no operation moved by 1% of the time
where the time goes in v8:
time: 37.5 us; the launch traced here: 37.3 us
  Pallas kernels  36.6 us (98%)
  local copies, waits for them, and re-layouts  0.66 us (2%)
    pallas_call x1, Pallas kernels, patch(): pl.pallas_call(functools.partial(patch_kernel, sizes), out_shape=pltpu.VM...  36.6 us

profile of v8, /device:TPU:7, one launch (start us, length us, event | category | flops | bytes accessed | tf_op | source)
XLA Modules:
  0.0 37.3 jit_solution(17969298580556797404)
XLA Ops:
  0.0 36.6 %shard_map.136 = bf16[1,128,512]{2,1,0:T(8,128)(2,1)S(1)} custom-call(s32[4]{0:T(128)} %refs_0_.1, s32[4]{0:T(128)} %refs_1_.1, s32[8]{0:T(128)} %refs_2_.1, f32[2]{0:T(128)} %refs_3_.1, bf16[1,128,512]{2,1,0:T(8,128)(2,1)} %refs_4_.1, bf16[2,128,1024]{2,1,0:T(8,128)(2,1)} %refs_5_.1, bf16[3,4,64]{2,1,0:T(4,128)(2,1)} %bitcast.2, ...), custom_call_target="tpu_custom_call" | custom-call | tf_op jit(solution)/shard_map/pallas_call | solution.py:719
  36.6 0.7 %copy.16 = bf16[1,128,512]{2,1,0:T(8,128)(2,1)} copy(bf16[1,128,512]{2,1,0:T(8,128)(2,1)S(1)} %shard_map.136) | data formatting | bytes 262144
